TPU v7x, 32 devices: a whole 2x2x4 slice. The times are simulated.
32 devices in a mesh: bins: 4 (over z), mp: 2 (over core), batch: 4 (over y, x).
Axes of the slice: x: 2, y: 2, z: 4, core: 2. Of those that a mesh axis runs over, the one named last changes fastest.
Arguments:
- signal: bfloat16 [64, 1024, 768], P('batch', 'bins', 'mp'), may hold values from -12 to 12
- segment_number_index: int32 [64, 1024], P('batch'), may hold values from 0 to 3, as said below
- cotangent: bfloat16 [64, 512, 768], P('batch', 'bins', 'mp'), may hold values from -12 to 12
- conv_wide: bfloat16 [5, 768, 768], P(None, None, 'mp'), may hold values from -0.09375 to 0.09375
- dilated_kernel_taps: bfloat16 [3, 768, 384], P(None, None, 'mp'), may hold values from -0.125 to 0.125
- pointwise: bfloat16 [384, 768], P(None, 'mp'), may hold values from -0.3125 to 0.3125
- gain_in: float32 [768], P('mp'), may hold values from 0.25 to 1.75
- shift_in: float32 [768], P('mp'), may hold values from -3 to 3
- gain_mid: float32 [768], P('mp'), may hold values from 0.25 to 1.75
- shift_mid: float32 [768], P('mp'), may hold values from -3 to 3
- hidden_norm_gain: float32 [384], P('mp'), may hold values from 0.25 to 1.75
- hidden_norm_bias: float32 [384], P('mp'), may hold values from -3 to 3
Outputs:
- output: bfloat16 [64, 512, 768], P('batch', 'bins', 'mp')
- grad_signal: float32 [64, 1024, 768], P('batch', 'bins', 'mp')
- grad_conv_wide: float32 [5, 768, 768], P(None, None, 'mp')
- dilated_kernel_gradient: float32 [3, 768, 384], P(None, None, 'mp')
- grad_pointwise: float32 [384, 768], P(None, 'mp')
- grad_gain_in: float32 [768], P('mp')
- grad_shift_in: float32 [768], P('mp')
- grad_gain_mid: float32 [768], P('mp')
- grad_shift_mid: float32 [768], P('mp')
- hidden_gain_gradient: float32 [384], P('mp')
- hidden_bias_gradient: float32 [384], P('mp')
Inputs may be any that keep to these rules, and one draw needn't show every extreme that they name: `segment_number_index`: each row holds four sequences 0, 1, 2, 3 in order; sequence j (j < 3) ends at an even bin within 64 bins of (j + 1) * 256.
All inputs are finite; a program needn't handle non-finite values.
Results may differ from a plain program's by a relative error of at most 0.017.
Values may be sent and summed in bfloat16 or wider, within the bound.
A program may use at most 192 MiB of HBM per device.

v0:
```python
import functools
import types

import jax
import jax.numpy as jnp
from jax import lax
from jax.experimental import pallas as pl
from jax.experimental.pallas import tpu as pltpu
from jax.sharding import PartitionSpec as P

DIL = 57
EPSILON = 1e-05
TAPS = 5
BF = jnp.bfloat16
F32 = jnp.float32
MESH = pl.DeviceIdType.MESH
K0 = 0.7978845608028654
K3 = 0.044715
ROWS = 8
VMEM_BYTES = 63 * 2**20


def gelu_up(x):
    t = jnp.tanh(x * (K0 + (K0 * K3) * (x * x)))
    h = 0.5 * x
    return h + h * t


def gelu_both(x):
    x2 = x * x
    t = jnp.tanh(x * (K0 + (K0 * K3) * x2))
    h = 0.5 * x
    return h + h * t, 0.5 + 0.5 * t + h * (1.0 - t * t) * (K0 + (3.0 * K0 * K3) * x2)


def dot(a, b, ca, cb):
    return lax.dot_general(a, b, (((ca,), (cb,)), ((), ())), preferred_element_type=F32)


def wide(mask, times):
    return jnp.concatenate([mask] * times, axis=1)


def al(x, n):
    return pl.multiple_of(x, n)


class Place:
    def __init__(self, nb, nm, na):
        self.nb, self.nm, self.na = nb, nm, na
        self.b = lax.axis_index("bins")
        self.m = lax.axis_index("mp")
        self.a = lax.axis_index("batch")
        self.layer = nm * na
        self.q = self.m * na + self.a

    def in_layer(self, q):
        return (self.b, q // self.na, lax.rem(q, self.na))

    def in_bins(self, b):
        return (b, self.m, self.a)

    @property
    def partner(self):
        return (self.b, 1 - self.m, self.a)

    def others(self, me, n):
        return [lax.rem(me + i, n) for i in range(1, n)]


def remote(src, dst, ss, rs, dev):
    return pltpu.make_async_remote_copy(
        src_ref=src, dst_ref=dst, send_sem=ss, recv_sem=rs, device_id=dev, device_id_type=MESH
    )


class Exchange:
    def __init__(self, buf, me, n, dev_of, ss, rs, others):
        self.buf, self.me, self.n, self.dev_of, self.ss, self.rs, self.others = (
            buf, me, n, dev_of, ss, rs, others,
        )

    def start(self, value):
        self.buf[self.me] = value
        for q in self.others:
            remote(self.buf.at[self.me], self.buf.at[self.me], self.ss.at[q], self.rs.at[self.me], self.dev_of(q)).start()

    def wait(self):
        for q in self.others:
            remote(self.buf.at[q], self.buf.at[q], self.ss.at[q], self.rs.at[q], self.dev_of(q)).wait_recv()
        return [self.buf[i] for i in range(self.n)]

    def drain(self):
        for q in self.others:
            remote(self.buf.at[self.me], self.buf.at[self.me], self.ss.at[q], self.rs.at[q], self.dev_of(q)).wait_send()


def merged(parts, count):
    means = [p[0:1] for p in parts]
    total = functools.reduce(jnp.add, means)
    mean = total / len(parts)
    squares = functools.reduce(jnp.add, [p[1:2] for p in parts])
    apart = functools.reduce(jnp.add, [(x - mean) * (x - mean) for x in means])
    return mean, squares + count * apart


def row_sum(x):
    return jnp.sum(x, axis=0, keepdims=True)


def greet(place):
    barrier = pltpu.get_barrier_semaphore()
    devices = [place.in_layer(q) for q in place.others(place.q, place.layer)]
    devices += [place.in_bins(b) for b in place.others(place.b, place.nb)]
    for d in devices:
        pl.semaphore_signal(barrier, inc=1, device_id=d, device_id_type=MESH)
    pl.semaphore_wait(barrier, len(devices))


PLAN = (
    ("bh", [18]),
    ("center", [18]),
    ("center2", [19]),
    ("rims", [18]),
    ("bm", [19, 15, 16, 17]),
    ("bm2", [18]),
    ("tap0", [19, 15, 16, 17]),
    ("tap1", [18, 0, 2]),
    ("tap2", [1]),
    ("tap3", [15, 16, 17, 4]),
    ("tap4", [3, 5]),
    ("tap5", [18, 1, 6, 8]),
    ("tap6", [19, 0, 15, 7]),
    ("tap7", [16, 2, 3, 10]),
    ("tap8", [17, 4, 5, 9, 11]),
    ("tap9", [1, 0, 15, 12, 14]),
    ("taps", [6, 7, 16, 13]),
    ("tile0", [2, 8, 4, 17]),
    ("tile1", [19]),
    ("tile2", [1, 9, 3, 0]),
    ("tile3", [11]),
    ("tile4", [10, 6, 2, 5]),
    ("tile5", [16, 4, 15]),
    ("tile6", [1, 13, 12]),
    ("tile7", [3, 8]),
    ("tile8", [0, 14, 6]),
    ("tile9", [7, 2, 19]),
    ("tile10", [17, 5, 10, 9, 4]),
    ("tile11", [11]),
    ("tile12", [3, 15, 8, 12, 16]),
    ("tile13", [6, 0]),
    ("tile14", [1, 7, 14, 13, 5, 2]),
    ("tile15", [10, 3]),
    ("end0", [9, 17, 11, 4, 0, 8, 6, 5, 12, 7, 1, 2, 14]),
    ("end1", [13, 3, 4, 10, 8, 9, 6, 11, 5, 7, 12, 10, 14, 8, 13, 9, 11, 7, 12, 10, 14, 13, 9, 12, 11, 14, 13]),
)


def main_body(dims, names, spans, *refs):
    nb, nm, na, T, S, CH, HC = dims
    C = 2 * CH
    HR = T * ROWS
    PR = S * ROWS
    rim = (DIL + 1) * ROWS
    r = types.SimpleNamespace(**dict(zip(names, refs, strict=True)))
    place = Place(nb, nm, na)
    b, m, a = place.b, place.m, place.a
    other = 1 - m
    total_in = float(HR * nb * nm * na)
    total_mid = float(PR * nb * nm * na)
    LANES = r.LANES
    RT = LANES.shape[0] // (C // 128)

    def part(name, at=0, n=None):
        pool, start, rows = spans[name]
        return getattr(r, pool).at[pl.ds(start + at, rows if n is None else n)]

    def local(src, dst, i):
        return pltpu.make_async_copy(src, dst, r.lsem.at[i])

    def cross(src, dst, i):
        return remote(src, dst, r.csem_s.at[i], r.csem_r.at[i], place.partner)

    RAW, STO, X, CT, HM = part("RAW"), part("STO"), part("X"), part("CT"), part("HM")
    H0, H1, W, PW, DT = part("H0"), part("H1"), part("W"), part("PW"), part("DT")
    COT = [part("COTR", 0, PR), part("COTR", PR, PR)]
    vectors = [r.v0, r.v1, r.v2, r.v3, r.v4, r.v5]
    PAR, SEG, SEGX, MASK, ST = r.PAR, r.SEG, r.SEGX, r.MASK, r.ST
    half = lambda at, n: pl.ds(al(at + m * n, n), n)

    sig, cot = r.sig, r.cot
    mine, theirs = pl.ds(al(m * HR, HR), HR), pl.ds(al(other * HR, HR), HR)
    raw_mine = r.N.at[pl.ds(al(spans["RAW"][1] + m * HR, 16), HR)]
    cot_mine = r.N.at[pl.ds(al(spans["COTR"][1] + m * PR, 16), PR)]
    lanes = pl.ds(al(m * CH, CH), CH)
    w0, pw0, dt0 = spans["W"][1], spans["PW"][1], spans["DT"][1]
    HH = HC // 2

    def weight(k):
        return r.M.at[pl.ds(w0 + k * C, C), lanes]

    def tap_rows(k):
        return r.M.at[pl.ds(al(dt0 + k * HC + m * HH, 16), HH)]

    pw_mine = r.M.at[pl.ds(pw0, HC), lanes]
    ld_sto = local(sig.at[theirs], STO, 0)
    ld_raw = local(sig.at[mine], raw_mine, 1)
    ld_seg = local(r.seg, SEG, 2)
    ld_w = [local(r.wide.at[k], weight(k), 3 + k) for k in range(TAPS)]
    ld_d = [local(r.taps.at[k], tap_rows(k), 8 + k) for k in range(3)]
    ld_pw = local(r.pw, pw_mine, 11)
    ld_cot = local(cot.at[pl.ds(al(m * PR, PR), PR)], cot_mine, 12)
    for c in [ld_sto, ld_raw, ld_seg, *ld_w, *ld_d, ld_pw, ld_cot]:
        c.start()
    for i in range(4):
        PAR[m, i : i + 1, :] = vectors[i][...].reshape(1, CH)
    for i in range(4, 6):
        PAR[m, i : i + 1, 0:HH] = vectors[i][...].reshape(1, HH)
    greet(place)
    x_sig = cross(sig.at[theirs], raw_mine, 0)
    x_par = cross(PAR.at[m], PAR.at[m], 1)
    x_w = [cross(r.wide.at[k], weight(k), 2 + k) for k in range(TAPS)]
    x_d = [cross(r.taps.at[k], tap_rows(k), 7 + k) for k in range(3)]
    x_pw = cross(r.pw, pw_mine, 10)
    x_cot = cross(cot.at[pl.ds(al(other * PR, PR), PR)], cot_mine, 11)
    crosses = [x_sig, x_par, *x_w, x_cot, x_pw, *x_d]
    for c in crosses:
        c.start()

    def exchange(i, name):
        return (
            Exchange(getattr(r, name + "A"), place.q, place.layer, place.in_layer, r.as_.at[i], r.ar_.at[i], place.others(place.q, place.layer)),
            Exchange(getattr(r, name + "B"), b, nb, place.in_bins, r.bs_.at[i], r.br_.at[i], place.others(b, nb)),
        )

    def finish_stats(ex, count):
        mean, squares = merged(ex[0].wait(), count)
        ex[1].start(jnp.concatenate([mean, squares], axis=0))
        return merged(ex[1].wait(), count * place.layer)

    def finish_sums(ex, between=lambda: None):
        ex[1].start(functools.reduce(jnp.add, ex[0].wait()))
        between()
        return functools.reduce(jnp.add, ex[1].wait())

    ex_in, ex_mid, ex_hid, ex_bh, ex_bm, ex_bi = exchanges = [
        exchange(i, n) for i, n in enumerate(["XI", "XM", "XH", "XG", "XD", "XS"])
    ]

    ps, pr, zs, zr = r.ps, r.pr, r.zs, r.zr
    N = r.N
    INNER = 4
    outer = nb // INNER
    inner = lax.rem(b, INNER)
    base = b - inner
    bits = (lax.rem(a, 2), a // 2)
    flip = ((b, m, a + 1 - 2 * bits[0]), (b, m, lax.rem(a + 2, 4)))
    early = outer == 1
    PSLOTS = spans["PS"][2] // C

    class Piece:
        def __init__(self, p, stack, lanes, first, n, R, F, full=False):
            self.p = p
            self.stack = stack
            self.lanes = pl.ds(*lanes)
            self.first = first
            self.n = n
            HALF, QUART = n // 2, n // 4
            self.SMALL = n // 16
            self.full = full
            self.steps = [0, 1, 2, 3, 5, 6] if full else [0, 1, 2, 3, 4, 5, 6]
            b1, b2 = bits[self.first], bits[1 - self.first]
            self.n1, self.n2 = flip[self.first], flip[1 - self.first]
            self.k1 = b1 * HALF
            self.s1 = (1 - b1) * HALF
            self.k2 = b1 * HALF + b2 * QUART
            self.s2 = b1 * HALF + (1 - b2) * QUART
            self.HALF, self.QUART = HALF, QUART
            self.R, self.F = R, F
            self.XB, self.YB, self.ZB = [spans[f"{x}{stack}"][1] for x in ("XB", "YB", "ZB")]

        def rows(self, start, at, n):
            return N.at[pl.ds(al(start + at, 16), n), self.lanes]

        def get(self, start, at, n):
            return N[pl.ds(al(start + at, 16), n), self.lanes].astype(F32)

        def put(self, start, at, n, v):
            N[pl.ds(al(start + at, 16), n), self.lanes] = v.astype(BF)

        def describe(self, make, i, dev):
            return lambda: remote(*make(), ps.at[self.p, i], pr.at[self.p, i], dev)

        def moves(self):
            F, R = self.F, self.R
            return {
                2: self.describe(lambda: (self.rows(R, self.s1, self.HALF), self.rows(self.XB, 0, self.HALF)), 2, self.n1),
                3: self.describe(lambda: (self.rows(R, self.s2, self.QUART), self.rows(self.YB, 0, self.QUART)), 3, self.n2),
                4: self.describe(lambda: (self.rows(F, self.k2, self.QUART),) * 2, 4, self.n2),
                5: self.describe(lambda: (self.rows(F, self.k1, self.HALF),) * 2, 5, self.n1),
            }

        def toward(self, which, i):
            j = lax.rem(inner + i, INNER)
            if self.full:
                src, dst = self.rows(self.R, self.k2, self.QUART), self.rows(self.ZB, inner * self.QUART, self.QUART)
            elif which == 0:
                src, dst = self.rows(self.R, self.k2 + j * self.SMALL, self.SMALL), self.rows(self.ZB, inner * self.SMALL, self.SMALL)
            else:
                src = dst = self.rows(self.F, self.k2 + inner * self.SMALL, self.SMALL)
            return remote(src, dst, zs.at[self.p, which, j], zr.at[self.p, which, inner], (base + j, m, a))

        def gather(self, which):
            for i in range(1, INNER):
                j = lax.rem(inner + i, INNER)
                if self.full:
                    ref = self.rows(self.ZB, j * self.QUART, self.QUART)
                else:
                    ref = self.rows(self.ZB, j * self.SMALL, self.SMALL) if which == 0 else self.rows(self.F, self.k2 + j * self.SMALL, self.SMALL)
                remote(ref, ref, zs.at[self.p, which, j], zr.at[self.p, which, j], (base + j, m, a)).wait_recv()

        def drain(self):
            for i in (2, 3, 4, 5):
                self.moves()[i]().wait_send()
            for which in range(1 if self.full else 2):
                for i in range(1, INNER):
                    self.toward(which, i).wait_send()
            if outer > 1:
                for i in range(1, outer):
                    self.outward(i).wait_send()
            self.out().wait()

        def outward(self, i):
            mine = b // INNER
            q = lax.rem(mine + i, outer)
            ref = r.F.at[self.slot(mine), self.lanes]
            return remote(ref, ref, r.os_.at[self.p, q], r.or_.at[self.p, mine], (q * INNER + inner, m, a))

        def slot(self, q):
            return pl.ds(al(spans[f"OB{self.stack}"][1] + q * self.SMALL, 8), self.SMALL)

        def out(self):
            k = self.stack
            to = r.oR.at[ORDER[k], :, self.lanes] if k < TAPS else r.oDP.at[pl.ds(self.F - dp_at, self.n), self.lanes]
            return local(self.rows(self.F, 0, self.n), to, 15 + self.p)

        def step(self, ph):
            p, moves = self.p, self.moves()
            HALF, QUART, SMALL = self.HALF, self.QUART, self.SMALL
            if ph == 0:
                moves[2]().start()
            elif ph == 1:
                moves[2]().wait_recv()
                self.put(self.R, self.k1, HALF, self.get(self.R, self.k1, HALF) + self.get(self.XB, 0, HALF))
                moves[3]().start()
            elif ph == 2:
                moves[3]().wait_recv()
                self.put(self.R, self.k2, QUART, self.get(self.R, self.k2, QUART) + self.get(self.YB, 0, QUART))
                for i in range(1, INNER):
                    self.toward(0, i).start()
            elif ph == 3:
                self.gather(0)
                n = QUART if self.full else SMALL
                at = self.k2 if self.full else self.k2 + inner * SMALL
                v = self.get(self.R, at, n)
                for i in range(1, INNER):
                    v += self.get(self.ZB, lax.rem(inner + i, INNER) * n, n)
                if outer > 1:
                    mine = b // INNER
                    r.F[self.slot(mine), self.lanes] = v
                    for i in range(1, outer):
                        self.outward(i).start()
                    for i in range(1, outer):
                        q = lax.rem(mine + i, outer)
                        ref = r.F.at[self.slot(q), self.lanes]
                        remote(ref, ref, r.os_.at[p, q], r.or_.at[p, q], (q * INNER + inner, m, a)).wait_recv()
                    v = r.F[self.slot(0), self.lanes]
                    for j in range(1, outer):
                        v += r.F[self.slot(j), self.lanes]
                self.put(self.F, at, n, v)
                if self.full:
                    moves[4]().start()
                else:
                    for i in range(1, INNER):
                        self.toward(1, i).start()
            elif ph == 4:
                self.gather(1)
                moves[4]().start()
            elif ph == 5:
                moves[4]().wait_recv()
                moves[5]().start()
            elif ph == 6:
                moves[5]().wait_recv()
                self.out().start()

    ORDER = (2, 1, 3, 0, 4)
    r_at, dp_at = spans["R"][1], spans["FD"][1]
    dps_at, dpr_at = spans["DPS"][1], r_at + TAPS * C
    thirds = [(q * CH // 3, CH // 3) for q in range(3)]
    pieces = []
    for k in range(TAPS + 1):
        for q in range(3):
            R, F = r_at + k * C, spans[f"F{k}"][1] if k < TAPS else dp_at
            pieces.append(Piece(len(pieces), k, thirds[q], (k + q) % 2, C, R, F))
    late = len(pieces)
    if early:
        pieces.append(Piece(late, 6, (0, CH), 0, CH, r_at + 6 * C, dp_at + C, True))
        pieces.append(Piece(late + 1, 7, (0, CH), 1, CH, r_at + 6 * C + CH, dp_at + C + CH, True))
    else:
        pieces.append(Piece(late, 6, (0, CH), 0, C, r_at + 6 * C, dp_at + C))

    class Share:
        def __init__(self, sem, src, dst, own, to, n):
            self.sem, self.src, self.dst, self.own, self.to, self.n = sem, src, dst, own, to, n

        def copy(self):
            at = lambda start: N.at[pl.ds(al(start, 16), self.n)]
            return remote(at(self.src), at(self.dst), r.shs.at[self.sem], r.shr.at[self.sem], place.partner)

        def sum(self):
            self.copy().wait_recv()
            v = self.own() + N[pl.ds(al(self.dst, 16), self.n), :].astype(F32)
            N[pl.ds(al(self.to, 16), self.n), :] = v.astype(BF)

    def dil_share(sem, at, n):
        own = lambda: N[pl.ds(dpr_at + at, n), :].astype(F32)
        return Share(sem, dps_at + at, dp_at + at, own, dpr_at + at, n)

    share_rest, share_pw, share_mid = dil_share(10, 0, C), dil_share(11, C, CH), dil_share(12, C + CH, CH)

    left = [list(pc.steps) for pc in pieces]
    plan = {}
    for name, which in PLAN:
        if not early:
            which = [p for p in which if p < len(pieces) and not (p == late and name in ("bh", "center", "center2"))]
        plan[name] = [(p, left[p].pop(0)) for p in which if left[p]]
    while any(left):
        first = max(len(x) for x in left)
        plan["end1"] += [(p, x.pop(0)) for p, x in enumerate(left) if len(x) == first]

    def pump(where):
        for p, ph in plan[where]:
            pieces[p].step(ph)

    ld_sto.wait()
    ld_raw.wait()
    CHK = 128
    raw_at = spans["RAW"][1] + m * HR

    def own_raw(i):
        return r.N[pl.ds(al(raw_at + i * CHK, 16), CHK), :].astype(F32).reshape(CHK // 8, 8, CH)

    def sto(i):
        return STO[pl.ds(al(i * CHK, CHK), CHK), :].astype(F32).reshape(CHK // 8, 8, CH)

    def s1(i, acc):
        return acc + jnp.sum(own_raw(i), axis=0) + jnp.sum(sto(i), axis=0)

    acc = lax.fori_loop(0, HR // CHK, s1, jnp.zeros((8, CH), F32))
    mean = row_sum(acc) / float(2 * HR)

    def s2(i, acc):
        u = own_raw(i) - mean
        v = sto(i) - mean
        return acc + jnp.sum(u * u, axis=0) + jnp.sum(v * v, axis=0)

    acc = lax.fori_loop(0, HR // CHK, s2, jnp.zeros((8, CH), F32))
    ex_in[0].start(jnp.concatenate([mean, row_sum(acc)], axis=0))

    ld_seg.wait()
    blocks = SEG.shape[1] // 128

    def make_segs(i, _):
        at = b * (T // 128) - 1 + i
        v = SEG[pl.ds(al(m * ROWS, ROWS), ROWS), pl.ds(al(jnp.clip(at, 0, blocks - 1) * 128, 128), 128)].astype(F32)
        v = jnp.where(jnp.logical_and(at >= 0, at < blocks), v, -1.0)
        for j in range(128):
            SEGX[pl.ds(al(i * 1024 + j * 8, 8), 8), :] = jnp.broadcast_to(v[:, j : j + 1], (8, 128))
        return 0

    lax.fori_loop(0, T // 128 + 2, make_segs, 0)
    BIN0 = 128 * 8

    def make_masks(i, _):
        mid = SEGX[pl.ds(al(i * 128 + BIN0, 128), 128), :]
        for j, o in enumerate((-2, -1, 1, 2)):
            off = SEGX[pl.ds(al(i * 128 + BIN0 + o * 8, 8), 128), :]
            MASK[j, pl.ds(al(i * 128, 128), 128), :] = jnp.where(off == mid, 1.0, 0.0).astype(BF)
        return 0

    lax.fori_loop(0, HR // 128, make_masks, 0)
    x_sig.wait_recv()
    BB = RT // ROWS

    def turn(src, dst, i):
        for h in range(2):
            for row in range(ROWS):
                v = src(h, row).astype(F32)
                for j in range(CH // 128):
                    LANES[pl.ds((h * (CH // 128) + j) * RT + row, BB, stride=ROWS), :] = v[:, j * 128 : (j + 1) * 128]
        for j in range(C // 128):
            dst[pl.ds(al(i * RT, RT), RT), j * 128 : (j + 1) * 128] = LANES[j * RT : (j + 1) * RT, :].astype(BF)

    def turn_x(i, _):
        turn(lambda h, row: RAW[pl.ds(al(h * HR + row * T + i * BB, BB), BB), :], X, i)
        return 0

    lax.fori_loop(0, T // BB, turn_x, 0)
    keep_x = local(X, r.oX, 13)
    keep_x.start()
    x_par.wait_recv()

    def vec(i):
        return jnp.concatenate([PAR[0, i : i + 1, :], PAR[1, i : i + 1, :]], axis=1)

    def hvec(i):
        return jnp.concatenate([PAR[0, i : i + 1, 0:HH], PAR[1, i : i + 1, 0:HH]], axis=1)

    la = ex_in[0].wait()
    n_own = float(2 * HR)
    lo = merged(la[0:na], n_own)
    hi = merged(la[na : 2 * na], n_own)
    ex_in[1].start(
        jnp.concatenate([jnp.concatenate([lo[0], hi[0]], axis=1), jnp.concatenate([lo[1], hi[1]], axis=1)], axis=0)
    )
    mu_in, sq = merged(ex_in[1].wait(), n_own * na)
    inv_in = lax.rsqrt(sq / total_in + EPSILON)
    gain_in, shift_in = vec(0), vec(1)
    scale_in = gain_in * inv_in
    ST[0:1, :] = mu_in
    ST[1:2, :] = inv_in
    ST[2:3, :] = gain_in
    HB = 256

    def make_hidden(i, last):
        at = al(i * HB, HB)
        pre = (X[pl.ds(at, HB), :].astype(F32) - mu_in) * scale_in + shift_in
        h = gelu_up(pre)
        H0[pl.ds(al(at + 16, 16), HB), :] = h.astype(BF)
        H1[pl.ds(at, HB), :] = jnp.concatenate([last, h[: HB - 8]], axis=0).astype(BF)
        return h[HB - 8 :]

    lax.fori_loop(0, HR // HB, make_hidden, jnp.zeros((8, C), F32))
    hs, hr = r.hs, r.hr
    down = (jnp.maximum(b - 1, 0), m, a)
    up = (jnp.minimum(b + 1, nb - 1), m, a)
    has_down, has_up = b > 0, b < nb - 1

    def when_down(f):
        pl.when(has_down)(f)

    def when_up(f):
        pl.when(has_up)(f)

    class Rims:
        def __init__(self, to_down, from_up, to_up, from_down, i):
            self.down = remote(to_down, from_up, hs.at[i], hr.at[i], down)
            self.up = remote(to_up, from_down, hs.at[i + 1], hr.at[i + 1], up)

        def start_down(self):
            when_down(self.down.start)

        def start_up(self):
            when_up(self.up.start)

        def wait_from_up(self):
            when_up(self.down.wait_recv)

        def wait_from_down(self):
            when_down(self.up.wait_recv)

        def drain(self):
            when_down(self.down.wait_send)
            when_up(self.up.wait_send)

    def clear_halo(ref):
        @pl.when(jnp.logical_not(has_down))
        def _():
            ref[0:16, :] = jnp.zeros((16, C), BF)

        @pl.when(jnp.logical_not(has_up))
        def _():
            ref[pl.ds(HR + 16, 16), :] = jnp.zeros((16, C), BF)

    def halos(ref, i):
        return Rims(ref.at[pl.ds(16, 16)], ref.at[pl.ds(HR + 16, 16)], ref.at[pl.ds(HR, 16)], ref.at[pl.ds(0, 16)], i)

    h_halo = halos(H0, 0)
    h_halo.start_down()
    h_halo.start_up()
    clear_halo(H0)

    def by_one_bin(even, odd):
        v = even[0:32, :].astype(F32)
        odd[0:16, :] = v[8:24].astype(BF)
        v = even[pl.ds(HR, 32), :].astype(F32)
        odd[pl.ds(HR, 16), :] = v[8:24].astype(BF)

    MJ = {-2: 0, -1: 1, 1: 2, 2: 3}

    def shifted(even, odd, o, at, n):
        if o % 2 == 0:
            v = even[pl.ds(al(at + (o + 2) * 8, 16), n), :]
        else:
            v = odd[pl.ds(al(at + (o + 1) * 8, 16), n), :]
        if o != 0:
            v = v * wide(MASK[MJ[o], pl.ds(al(at, 16), n), :], C // 128)
        return v

    def w(k):
        return W[k * C : (k + 1) * C, :]

    def put_lanes(v, n):
        for j in range(C // 128):
            LANES[j * RT : j * RT + n, :] = v[:, j * 128 : (j + 1) * 128]

    def get_lanes(at, n):
        return jnp.concatenate([LANES[pl.ds(al(j * RT + at, 8), n), :] for j in range(C // 128)], axis=1)

    for c in (*ld_w,):
        c.wait()
    for c in x_w:
        c.wait_recv()
    POOL, DIFF, SUM = r.POOL, r.DIFF, r.SUM
    SUM[...] = jnp.zeros_like(SUM)

    def conv_tile(i):
        at = al(i * RT, RT)
        acc = None
        for k in range(TAPS):
            d = dot(shifted(H0, H1, k - 2, at, RT), w(k), 1, 0)
            acc = d if acc is None else acc + d
        put_lanes(acc, RT)

        def pool(j, s):
            v = get_lanes(j * 128, 128).reshape(8, 2, 8, C)
            c0, c1 = v[:, 0], v[:, 1]
            d = c0 - c1
            p = jnp.maximum(c0, c1) + jnp.log(1.0 + jnp.exp(-jnp.abs(d)))
            to = pl.ds(al(i * (RT // 2) + j * 64, 64), 64)
            POOL[to, :] = p.reshape(64, C)
            DIFF[to, :] = d.reshape(64, C)
            return s + jnp.sum(p, axis=0)

        SUM[...] += lax.fori_loop(0, RT // 128, pool, jnp.zeros((8, C), F32))

    NT = HR // RT

    def conv_loop(i, _):
        conv_tile(i)
        return 0

    lax.fori_loop(1, NT - 1, conv_loop, 0)
    h_halo.wait_from_up()
    h_halo.wait_from_down()
    by_one_bin(H0, H1)
    lax.fori_loop(0, 2, lambda i, _: (conv_tile(i * (NT - 1)), 0)[1], 0)

    mean = row_sum(SUM[...]) / float(PR)

    def m2_mid(i, acc):
        v = POOL[pl.ds(al(i * 128, 128), 128), :].reshape(16, 8, C) - mean
        return acc + jnp.sum(v * v, axis=0)

    acc = lax.fori_loop(0, PR // 128, m2_mid, jnp.zeros((8, C), F32))
    ex_mid[0].start(jnp.concatenate([mean, row_sum(acc)], axis=0))

    ld_cot.wait()
    x_cot.wait_recv()

    def turn_ct(i, _):
        turn(lambda h, row: COT[h][pl.ds(al(row * S + i * BB, BB), BB), :], CT, i)
        return 0

    lax.fori_loop(0, S // BB, turn_ct, 0)
    ld_pw.wait()
    x_pw.wait_recv()
    GT, DO, E0 = part("GT"), part("DO"), part("E0")
    E1, GML = part("GM"), [part("GM", 0, PR), part("GM", PR, PR)]

    def make_gt(i, _):
        at = pl.ds(al(i * 256, 256), 256)
        GT[at, :] = dot(CT[at, :], PW[...], 1, 1)
        return 0

    lax.fori_loop(0, PR // 256, make_gt, 0)
    for c in ld_d:
        c.wait()
    for c in x_d:
        c.wait_recv()

    def dt(k):
        return DT[k * HC : (k + 1) * HC, :]

    mu_mid, sq = finish_stats(ex_mid, float(PR))
    inv_mid = lax.rsqrt(sq / total_mid + EPSILON)
    gain_mid, shift_mid = vec(2), vec(3)
    scale_mid = gain_mid * inv_mid

    def make_mid(i, _):
        at = pl.ds(al(i * 128, 128), 128)
        HM[at, :] = gelu_up((POOL[at, :] - mu_mid) * scale_mid + shift_mid).astype(BF)
        return 0

    lax.fori_loop(0, PR // 128, make_mid, 0)

    RS = [part("RS", 0, rim), part("RS", rim, rim)]
    RR = [part("RR", 0, rim), part("RR", rim, rim)]
    p_rims = Rims(RS[1], RR[1], RS[0], RR[0], 2)
    QR = PR // 4
    e0_at, e1_at, do_at, hm_at = spans["E0"][1], spans["GM"][1], spans["DO"][1], spans["HM"][1]

    def pick(i, table):
        v = jnp.int32(table[-1])
        for n in range(len(table) - 2, -1, -1):
            v = jnp.where(i == n, table[n], v)
        return v

    quarter = (3, 2, 0, 1, 0, 1, 2, 3, 0, 1, 2, 3)
    taps_of = (0, 0, 2, 2, 0, 0, 2, 2, 1, 1, 1, 1)
    starts = [{0: e0_at + rim, 1: do_at, 2: e1_at}[k] + q * QR for k, q in zip(taps_of, quarter)]

    def product(i, _):
        v = dot(
            r.M[pl.ds(al(hm_at + pick(i, quarter) * QR, 16), QR), :],
            r.M[pl.ds(al(dt0 + pick(i, taps_of) * HC, 16), HC), :],
            1, 1,
        )
        r.F[pl.ds(al(pick(i, starts), 8), QR), :] = v

        @pl.when(i == 1)
        def _():
            RS[0][...] = E0[PR : PR + rim, :].astype(BF)
            p_rims.start_up()

        @pl.when(i == 3)
        def _():
            RS[1][...] = E1[0:rim, :].astype(BF)
            p_rims.start_down()

        return 0

    lax.fori_loop(0, len(quarter), product, 0)

    def take_rims(rims, low, high):
        rims.wait_from_down()
        rims.wait_from_up()

        @pl.when(has_down)
        def _():
            low[...] = RR[0][...].astype(F32)

        @pl.when(jnp.logical_not(has_down))
        def _():
            low[...] = jnp.zeros((rim, HC), F32)

        @pl.when(has_up)
        def _():
            high[...] = RR[1][...].astype(F32)

        @pl.when(jnp.logical_not(has_up))
        def _():
            high[...] = jnp.zeros((rim, HC), F32)

    take_rims(p_rims, part("E0", 0, rim), part("GM", PR, rim))

    def same(i, by):
        def pick(off):
            return SEGX[pl.ds(al(i * 256 + BIN0 + off * 16, 16), 256), :].reshape(16, 2, 8, 128)[:, 0]

        return wide(jnp.where(pick(0) == pick(by), 1.0, 0.0).reshape(128, 128), HC // 128)

    def add_dil(i, s):
        at = pl.ds(al(i * 128, 128), 128)
        v = DO[at, :]
        v += same(i, -DIL) * E0[pl.ds(al(i * 128 + 8, 8), 128), :]
        v += same(i, DIL) * E1[pl.ds(al(i * 128 + DIL * 8, 8), 128), :]
        DO[at, :] = v
        return s + jnp.sum(v.reshape(16, 8, HC), axis=0)

    acc = lax.fori_loop(0, PR // 128, add_dil, jnp.zeros((8, HC), F32))
    mean = row_sum(acc) / float(PR)

    def m2_hid(i, acc):
        v = DO[pl.ds(al(i * 128, 128), 128), :].reshape(16, 8, HC) - mean
        return acc + jnp.sum(v * v, axis=0)

    acc = lax.fori_loop(0, PR // 128, m2_hid, jnp.zeros((8, HC), F32))
    ex_hid[0].start(jnp.concatenate([mean, row_sum(acc)], axis=0))
    mu_hid, sq = finish_stats(ex_hid, float(PR))
    inv_hid = lax.rsqrt(sq / total_mid + EPSILON)
    gain_hid, shift_hid = hvec(4), hvec(5)
    HT = part("HT")

    def make_top(i, s):
        at = pl.ds(al(i * 128, 128), 128)
        xhat = (DO[at, :] - mu_hid) * inv_hid
        h, slope = gelu_both(xhat * gain_hid + shift_hid)
        HT[at, :] = h.astype(BF)
        da = slope * GT[at, :]
        GT[at, :] = da
        DO[at, :] = xhat
        return (
            s[0] + jnp.sum((da * xhat).reshape(16, 8, HC), axis=0),
            s[1] + jnp.sum(da.reshape(16, 8, HC), axis=0),
        )

    zero = jnp.zeros((8, HC), F32)
    sg, sb = lax.fori_loop(0, PR // 128, make_top, (zero, zero))
    ex_bh[0].start(jnp.concatenate([row_sum(sg), row_sum(sb)], axis=0))

    OB = 256

    def make_out(i, _):
        at = pl.ds(al(i * OB, OB), OB)
        v = (POOL[at, :] + dot(HT[at, :], PW[...], 1, 0)).astype(BF)
        COT[0][at, :] = v[:, :CH]
        COT[1][at, :] = v[:, CH:]
        return 0

    lax.fori_loop(0, PR // OB, make_out, 0)
    cot_other = r.N.at[pl.ds(al(spans["COTR"][1] + other * PR, 16), PR)]
    o_own = local(cot_mine, r.oOUT.at[m], 14)
    o_own.start()
    o_cross = cross(cot_other, r.oOUT.at[m], 12)
    o_cross.start()
    gp = dot(HT[...], CT[...], 0, 0)
    N[dpr_at + C : dpr_at + C + HC, :] = jnp.where(m == 0, gp[:, :CH], gp[:, CH:]).astype(BF)
    N[dps_at + C : dps_at + C + HC, :] = jnp.where(m == 0, gp[:, CH:], gp[:, :CH]).astype(BF)
    share_pw.copy().start()

    v = finish_sums(ex_bh, lambda: (share_pw.sum(), pump("bh")))
    ST[8:10, 0:HC] = v
    ST[8:10, HC:] = jnp.zeros((2, C - HC), F32)
    scale = gain_hid * inv_hid
    mg, mb = v[0:1] / total_mid, v[1:2] / total_mid
    GD = [part("GD", k * PR, PR) for k in range(3)]

    def make_gd(i, _):
        at = pl.ds(al(i * 128, 128), 128)
        g = (scale * (GT[at, :] - mb - DO[at, :] * mg)).astype(BF)
        GD[1][at, :] = g
        E0[pl.ds(al(i * 128 + rim, 16), 128), :] = g.astype(F32)
        return 0

    lax.fori_loop(0, PR // 128, make_gd, 0)
    p_rims.drain()
    g_rims = Rims(part("GD", PR, rim), RR[1], part("GD", 2 * PR - rim, rim), RR[0], 4)
    g_rims.start_up()
    g_rims.start_down()


    def to_gm(make, add):
        def body(i, _):
            at = pl.ds(al(i * QR, QR), QR)
            v = make(at)
            for h in range(2):
                u = v[:, h * CH : (h + 1) * CH]
                GML[h][at, :] = GML[h][at, :] + u if add else u
            return 0

        lax.fori_loop(0, 4, body, 0)

    to_gm(lambda at: dot(GD[1][at, :], dt(1), 1, 0), False)
    gd_at = spans["GD"][1]

    def dil_grad(k, to):
        g = dot(N[pl.ds(al(gd_at + k * PR, 16), PR), :], HM[...], 0, 0)
        own = jnp.where(m == 0, g[:HH], g[HH:]).astype(BF)
        for_partner = jnp.where(m == 0, g[HH:], g[:HH]).astype(BF)
        for h in range(2):
            at = to + h * HH
            N[pl.ds(al(dpr_at + at, 16), HH), :] = own[:, h * CH : (h + 1) * CH]
            N[pl.ds(al(dps_at + at, 16), HH), :] = for_partner[:, h * CH : (h + 1) * CH]

    dil_grad(1, C + CH)
    share_mid.copy().start()
    pump("center")
    share_mid.sum()
    pump("center2")
    take_rims(g_rims, part("E0", 0, rim), part("E0", PR + rim, rim))
    pump("rims")

    def mask_gd(i, _):
        at = pl.ds(al(i * 128, 128), 128)
        GD[0][at, :] = (same(i, DIL) * E0[pl.ds(al(i * 128 + rim + DIL * 8, 8), 128), :]).astype(BF)
        GD[2][at, :] = (same(i, -DIL) * E0[pl.ds(al(i * 128 + rim - DIL * 8, 8), 128), :]).astype(BF)
        return 0

    lax.fori_loop(0, PR // 128, mask_gd, 0)
    to_gm(lambda at: dot(GD[0][at, :], dt(0), 1, 0) + dot(GD[2][at, :], dt(2), 1, 0), True)

    def gm(at):
        return jnp.concatenate([GML[0][at, :], GML[1][at, :]], axis=1)

    def make_dmid(i, s):
        at = pl.ds(al(i * 64, 64), 64)
        xhat = (POOL[at, :] - mu_mid) * inv_mid
        _, slope = gelu_both(xhat * gain_mid + shift_mid)
        da = slope * gm(at)
        GML[0][at, :] = da[:, :CH]
        GML[1][at, :] = da[:, CH:]
        return (
            s[0] + jnp.sum((da * xhat).reshape(8, 8, C), axis=0),
            s[1] + jnp.sum(da.reshape(8, 8, C), axis=0),
        )

    zero = jnp.zeros((8, C), F32)
    sg, sb = lax.fori_loop(0, PR // 64, make_dmid, (zero, zero))
    g_rims.drain()
    o_own.wait()
    o_cross.wait_send()
    keep_x.wait()
    ex_bm[0].start(jnp.concatenate([row_sum(sg), row_sum(sb)], axis=0))

    lax.fori_loop(0, 2, lambda i, _: (dil_grad(2 * i, i * CH), 0)[1], 0)
    share_rest.copy().start()
    v = finish_sums(ex_bm, lambda: (share_rest.sum(), pump("bm")))
    ST[6:8, :] = v
    mg, mb = v[0:1] / total_mid, v[1:2] / total_mid
    pump("bm2")
    GC0, GC1 = part("GC0"), H1

    def make_gc(i, last):
        at = pl.ds(al(i * 64, 64), 64)
        xhat = (POOL[at, :] - mu_mid) * inv_mid
        g = CT[at, :].astype(F32) + scale_mid * (gm(at) - mb - xhat * mg)
        d = DIFF[at, :]
        e = jnp.exp(-jnp.abs(d))
        big = 1.0 / (1.0 + e)
        small = e * big
        g0 = g * jnp.where(d >= 0, big, small)
        g1 = g * jnp.where(d >= 0, small, big)
        v = jnp.stack([g0.reshape(8, 8, C), g1.reshape(8, 8, C)], axis=1).reshape(128, C)
        GC0[pl.ds(al(i * 128 + 16, 16), 128), :] = v.astype(BF)
        GC1[pl.ds(al(i * 128, 128), 128), :] = jnp.concatenate([last, v[:120]], axis=0).astype(BF)
        return v[120:]

    lax.fori_loop(0, PR // 64, make_gc, jnp.zeros((8, C), F32))
    g_halo = halos(GC0, 6)
    g_halo.start_down()
    g_halo.start_up()
    clear_halo(GC0)
    XX = part("XX")
    back_x = local(r.oX, XX, 13)

    own_at = spans["GM"][1]
    h0_at = spans["H0"][1] + 16
    ps_at = spans["PS"][1]
    HALF = C // 2
    first_half = (1 - bits[0]) * HALF

    def tap_share(i, j):
        at = first_half if j == 0 else HALF - first_half
        own = lambda: r.F[pl.ds(al(own_at + i % 2 * PR + at, 8), HALF), :]
        return Share(2 * i + j, ps_at + i % PSLOTS * C + at, spans[f"F{i}"][1] + at, own, r_at + i * C + at, HALF)

    shares = [tap_share(i, j) for i in range(TAPS) for j in range(2)]

    def masked(k):
        def body(j, _):
            XX[pl.ds(al(j * 256, 256), 256), :] = shifted(GC0, GC1, 2 - k, j * 256, 256)
            return 0

        lax.fori_loop(0, HR // 256, body, 0)

    def half_tap(it, _):
        i, j = it // 2, lax.rem(it, 2)
        for n in range(TAPS):

            @pl.when(it == 2 * n)
            def _(n=n):
                if n == 1:
                    g_halo.wait_from_up()
                    g_halo.wait_from_down()
                    by_one_bin(GC0, GC1)
                if n >= PSLOTS:
                    for c in shares[2 * (n - PSLOTS) : 2 * (n - PSLOTS) + 2]:
                        c.copy().wait_send()
                masked(ORDER[n])

        odd = lax.rem(i, 2)
        at = jnp.where(j == 0, first_half, HALF - first_half)
        v = dot(r.M[h0_at : h0_at + HR, pl.ds(al(at, 128), HALF)], XX[...], 0, 0)
        r.F[pl.ds(al(own_at + odd * PR + at, 8), HALF), :] = jnp.where(m == 0, v[:, :CH], v[:, CH:])
        N[pl.ds(al(ps_at + lax.rem(i, PSLOTS) * C + at, 16), HALF), :] = jnp.where(m == 0, v[:, CH:], v[:, :CH]).astype(BF)
        for n in range(2 * TAPS):

            @pl.when(it == n)
            def _(n=n):
                shares[n].copy().start()
                if n:
                    shares[n - 1].sum()
                pump(f"tap{n}")

        return 0

    lax.fori_loop(0, 2 * TAPS, half_tap, 0)
    shares[-1].sum()
    pump("taps")

    back_x.start()
    for c in shares[2 * (TAPS - PSLOTS) :]:
        c.copy().wait_send()
    mu, inv, gain, shift = ST[0:1, :], ST[1:2, :], gain_in, shift_in
    RB = 256
    DA = [part("RAW", 0, HR), part("RAW", HR, HR)]

    def tile(i, s):
        at = i * RB
        acc = None
        for k in range(TAPS):
            d = dot(shifted(GC0, GC1, 2 - k, at, RB), w(k), 1, 1)
            acc = d if acc is None else acc + d
        put_lanes(acc, RB)
        for n in range(HR // RB):

            @pl.when(i == n)
            def _(n=n):
                pump(f"tile{2 * n}")
                if n == 0:
                    back_x.wait()


        def back(j, s):
            to = pl.ds(al(at + j * 64, 64), 64)
            xhat = (XX[to, :].astype(F32) - mu) * inv
            _, slope = gelu_both(xhat * gain + shift)
            da = slope * get_lanes(j * 64, 64)
            DA[0][to, :] = da[:, :CH].astype(BF)
            DA[1][to, :] = da[:, CH:].astype(BF)
            return (
                s[0] + jnp.sum((da * xhat).reshape(8, 8, C), axis=0),
                s[1] + jnp.sum(da.reshape(8, 8, C), axis=0),
            )

        s = lax.fori_loop(0, RB // 64, back, s)
        for n in range(HR // RB):

            @pl.when(i == n)
            def _(n=n):
                pump(f"tile{2 * n + 1}")

        return s

    s = lax.fori_loop(0, HR // RB, tile, (zero, zero))
    ex_bi[0].start(jnp.concatenate([row_sum(s[0]), row_sum(s[1])], axis=0))
    d_own = local(raw_mine, r.oDA.at[m], 12)
    d_own.start()
    d_cross = cross(r.N.at[pl.ds(al(spans["RAW"][1] + other * HR, 16), HR)], r.oDA.at[m], 13)
    d_cross.start()
    pump("end0")
    ex_bi[1].start(functools.reduce(jnp.add, ex_bi[0].wait()))
    pump("end1")
    ST[4:6, :] = functools.reduce(jnp.add, ex_bi[1].wait())
    ST[3:4, :] = jnp.zeros((1, C), F32)
    ST[10:16, :] = jnp.zeros((6, C), F32)
    o_st = local(ST, r.oST, 14)
    o_st.start()
    for pc in pieces:
        pc.drain()
    for c in (share_rest, share_pw, share_mid):
        c.copy().wait_send()
    d_own.wait()
    o_st.wait()
    d_cross.wait()
    o_cross.wait_recv()
    for c in crosses:
        c.wait_send()
    for e in exchanges:
        e[0].drain()
        e[1].drain()
    h_halo.drain()
    g_halo.drain()


def call_main(axes, sig, seg, cot, wide_taps, taps, pw, vectors):
    nb, nm, na = axes
    CH = sig.shape[1]
    C = 2 * CH
    HC = pw.shape[0]
    assert HC == CH
    HR = sig.shape[0] // 2
    PR = cot.shape[0] // 2
    T, S = HR // ROWS, PR // ROWS
    rim = (DIL + 1) * ROWS
    RT = 512
    NA = nm * na
    early = nb == 4
    NP = 3 * (TAPS + 1) + (2 if early else 1)
    inputs = dict(sig=sig, seg=seg, cot=cot, wide=wide_taps, taps=taps, pw=pw)
    inputs.update({f"v{i}": v for i, v in enumerate(vectors)})
    sd = jax.ShapeDtypeStruct
    outs = dict(
        oX=sd((HR, C), BF),
        oDA=sd((2, HR, CH), BF),
        oOUT=sd((2, PR, CH), BF),
        oR=sd((TAPS, C, CH), BF),
        oDP=sd((2 * C, CH), BF),
        oST=sd((16, C), F32),
    )
    spans = {}

    def lay(pool, start, items):
        for name, n in items:
            spans[name] = (pool, start, n)
            start += n
        return start

    end = lay("N", 0, [("RAW", 2 * HR), ("STO", HR), ("COTR", 2 * PR), ("HT", PR), ("RS", 2 * rim), ("RR", 2 * rim)])
    lay("N", spans["STO"][1], [("DPS", 2 * C)])
    lay("N", spans["COTR"][1], [(f"XB{p}", C // 2) for p in range(TAPS)])
    lay("N", spans["HT"][1], [(f"YB{p}", C // 4) for p in range(TAPS)])
    lay("N", spans["RS"][1], [(f"F{p}", C) for p in range(2)])
    end = lay("N", end, [("GD", 3 * PR)])
    lay("N", spans["GD"][1], [("R", (TAPS + 2) * C)])
    end = max(end, spans["R"][1] + (TAPS + 2) * C)
    end = lay("N", end, [(f"F{p}", C) for p in range(2, TAPS)] + [("FD", 2 * C)])
    lay("N", spans["RAW"][1] + HR, [("PS", 2 * C)])
    sizes = {p: C for p in range(TAPS + 1)} | ({6: CH, 7: CH} if early else {6: C})
    rest = range(TAPS, len(sizes))
    end = lay("N", end, [(f"XB{p}", sizes[p] // 2) for p in rest] + [(f"YB{p}", sizes[p] // 4) for p in rest])
    n_rows = lay("N", end, [(f"ZB{p}", C // 2 if p > 5 and early else C // 4) for p in range(len(sizes))])
    end = lay("M", 0, [("X", HR), ("gap", 32), ("HM", PR), ("CT", PR), ("H0", HR + 32), ("H1", HR + 32)])
    lay("M", 0, [("GC0", HR + 32)])
    lay("M", spans["HM"][1], [("XX", HR)])
    m_rows = lay("M", end, [("W", TAPS * C), ("PW", HC), ("DT", 3 * HC)])
    f_rows = lay("F", 0, [("E0", PR + 2 * rim), ("GM", 2 * PR), ("DO", PR), ("GT", PR)])
    V = pltpu.VMEM
    DMA = pltpu.SemaphoreType.DMA
    scratch = dict(
        N=V((n_rows, CH), BF),
        M=V((m_rows, C), BF),
        F=V((f_rows, CH), F32),
        LANES=V((C // 128 * RT, 128), F32),
        MASK=V((4, HR, 128), BF),
        SEG=V(seg.shape, jnp.int32),
        SEGX=V(((T + 256) * ROWS, 128), F32),
        PAR=V((2, 8, CH), F32),
        ST=V((16, C), F32),
        SUM=V((8, C), F32),
        POOL=V((PR, C), F32),
        DIFF=V((PR, C), F32),
        XIA=V((NA, 2, CH), F32), XIB=V((nb, 2, C), F32),
        XMA=V((NA, 2, C), F32), XMB=V((nb, 2, C), F32),
        XHA=V((NA, 2, HC), F32), XHB=V((nb, 2, HC), F32),
        XGA=V((NA, 2, HC), F32), XGB=V((nb, 2, HC), F32),
        XDA=V((NA, 2, C), F32), XDB=V((nb, 2, C), F32),
        XSA=V((NA, 2, C), F32), XSB=V((nb, 2, C), F32),
        lsem=DMA((15 + NP,)),
        shs=DMA((13,)), shr=DMA((13,)),
        csem_s=DMA((14,)), csem_r=DMA((14,)),
        as_=DMA((6, NA)), ar_=DMA((6, NA)),
        bs_=DMA((6, nb)), br_=DMA((6, nb)),
        hs=DMA((8,)), hr=DMA((8,)),
        ps=DMA((NP, 6)), pr=DMA((NP, 6)),
        zs=DMA((NP, 2, 4)), zr=DMA((NP, 2, 4)),
    )
    outer = nb // 4
    if outer > 1:
        scratch.update(os_=DMA((NP, outer)), or_=DMA((NP, outer)))
        n = outer * (C // 16)
        assert lay("F", spans["E0"][1], [(f"OB{p}", n) for p in range(TAPS)]) <= spans["GM"][1]
        assert lay("F", spans["DO"][1], [(f"OB{p}", n) for p in range(TAPS, TAPS + 2)]) <= f_rows
    names = list(inputs) + list(outs) + list(scratch)
    anyspec = pl.BlockSpec(memory_space=pl.ANY)
    vmem = pl.BlockSpec(memory_space=pltpu.VMEM)
    res = pl.pallas_call(
        functools.partial(main_body, (nb, nm, na, T, S, CH, HC), names, spans),
        out_shape=list(outs.values()),
        in_specs=[vmem if n.startswith("v") else anyspec for n in inputs],
        out_specs=[anyspec] * len(outs),
        scratch_shapes=list(scratch.values()),
        compiler_params=pltpu.CompilerParams(
            collective_id=0, has_side_effects=True, vmem_limit_bytes=VMEM_BYTES
        ),
        cost_estimate=pl.CostEstimate(flops=44_000_000_000, bytes_accessed=40_000_000, transcendentals=8_000_000),
        name="forward_and_backward",
    )(*inputs.values())
    return dict(zip(outs, res, strict=True))


def last_body(dims, sig, da, out, rr, dk0, dk1, pw, stats, gs_ref, out_ref, gw_ref, dk_ref, pw_ref,
              g0, g1, g2, g3, g4, g5, lanes, lanes2):
    CH, total_in = dims
    m = lax.axis_index("mp")
    step = pl.program_id(0)
    n = da.shape[1]
    BB = n // ROWS
    v = da[0].astype(F32)
    u = out[0].astype(F32)
    n2 = out.shape[1]
    B2 = n2 // ROWS
    for j in range(CH // 128):
        lanes[j * n : (j + 1) * n, :] = v[:, j * 128 : (j + 1) * 128]
        lanes2[j * n2 : (j + 1) * n2, :] = u[:, j * 128 : (j + 1) * 128]
    st = stats[:, pl.ds(al(m * CH, CH), CH)]
    mu, inv, gain, gg, gb = [st[i : i + 1] for i in (0, 1, 2, 4, 5)]
    scale = gain * inv
    mg, mb = gg / total_in, gb / total_in
    for row in range(ROWS):
        for j in range(CH // 128):
            c = slice(j * 128, (j + 1) * 128)
            d = lanes[pl.ds(j * n + row, BB, stride=ROWS), :]
            xhat = (sig[row, :, c].astype(F32) - mu[:, c]) * inv[:, c]
            gs_ref[row, :, c] = scale[:, c] * (d - mb[:, c] - xhat * mg[:, c])
            out_ref[row, :, c] = lanes2[pl.ds(j * n2 + row, B2, stride=ROWS), :].astype(BF)
    gw_ref[...] = rr[...].astype(F32)
    dk_ref[...] = jnp.concatenate([dk0[...].astype(F32), dk1[...].astype(F32)], axis=1)
    pw_ref[...] = pw[...].astype(F32)

    @pl.when(step == 0)
    def _():
        for ref, i in ((g0, 4), (g1, 5), (g2, 6), (g3, 7)):
            ref[...] = st[i : i + 1].reshape(CH)
        HH = g4.shape[0]
        hid = stats[8:10, : 2 * HH]
        hid = jnp.where(m == 0, hid[:, :HH], hid[:, HH:])
        g4[...] = hid[0:1].reshape(HH)
        g5[...] = hid[1:2].reshape(HH)


def call_last(axes, sig, o):
    nb, nm, na = axes
    rows, T, CH = sig.shape
    S = T // 2
    C = 2 * CH
    HC = CH
    HH = HC // 2
    NC = 4
    steps = 2 * NC
    sd = jax.ShapeDtypeStruct
    total_in = float(rows * T * nb * na)
    rr = o["oR"].reshape(-1, CH)
    dp = o["oDP"]
    flat = lambda n, w: pl.BlockSpec((n, w), lambda i: (i, 0))
    whole1 = pl.BlockSpec(memory_space=pltpu.VMEM)
    nr, npw, nd = rr.shape[0] // steps, HC // steps, HH
    tap_of = lambda i: jnp.minimum(i // 2, 2)
    base = lambda i: jnp.where(tap_of(i) == 1, 6, tap_of(i))
    return pl.pallas_call(
        functools.partial(last_body, (CH, total_in)),
        grid=(steps,),
        out_shape=[
            sd((rows, T, CH), F32),
            sd((rows, S, CH), BF),
            sd(rr.shape, F32),
            sd((3 * HH, C), F32),
            sd((HC, CH), F32),
            *[sd((CH,), F32)] * 4,
            *[sd((HH,), F32)] * 2,
        ],
        in_specs=[
            pl.BlockSpec((ROWS, T // NC, CH), lambda i: (i // NC, i % NC, 0)),
            pl.BlockSpec((1, T * ROWS // NC, CH), lambda i: (i // NC, i % NC, 0)),
            pl.BlockSpec((1, S * ROWS // NC, CH), lambda i: (i // NC, i % NC, 0)),
            flat(nr, CH),
            pl.BlockSpec((nd, CH), lambda i: (base(i), 0)),
            pl.BlockSpec((nd, CH), lambda i: (base(i) + 1, 0)),
            pl.BlockSpec((npw, CH), lambda i: (4 * HH // npw + i, 0)),
            pl.BlockSpec((16, C), lambda i: (0, 0)),
        ],
        out_specs=[
            pl.BlockSpec((ROWS, T // NC, CH), lambda i: (i // NC, i % NC, 0)),
            pl.BlockSpec((ROWS, S // NC, CH), lambda i: (i // NC, i % NC, 0)),
            flat(nr, CH),
            pl.BlockSpec((nd, C), lambda i: (tap_of(i), 0)),
            flat(npw, CH),
            *[pl.BlockSpec((CH,), lambda i: (0,))] * 4,
            *[pl.BlockSpec((HH,), lambda i: (0,))] * 2,
        ],
        scratch_shapes=[
            pltpu.VMEM((CH // 128 * T * ROWS // NC, 128), F32),
            pltpu.VMEM((CH // 128 * S * ROWS // NC, 128), F32),
        ],
        compiler_params=pltpu.CompilerParams(vmem_limit_bytes=VMEM_BYTES),
        name="last_pass",
    )(sig, o["oDA"], o["oOUT"], rr, dp, dp, dp, o["oST"])


def on_device(axes, signal, seg, cotangent, conv_wide, taps, pointwise, *vectors):
    CH = signal.shape[2]
    o = call_main(
        axes, signal.reshape(-1, CH), seg, cotangent.reshape(-1, CH), conv_wide, jnp.swapaxes(taps, 1, 2), pointwise, vectors
    )
    gs, out, gw, dk, pw, *small = call_last(axes, signal, o)
    K, C, HH = taps.shape
    return (out, gs, gw.reshape(conv_wide.shape), jnp.swapaxes(dk.reshape(K, HH, C), 1, 2), pw, *small)


def solution(mesh):
    axes = (mesh.shape["bins"], mesh.shape["mp"], mesh.shape["batch"])
    cut = P("batch", "bins", "mp")
    tap = P(None, None, "mp")
    return jax.shard_map(
        functools.partial(on_device, axes),
        mesh=mesh,
        in_specs=(cut, P("batch", None), cut, tap, tap, P(None, "mp")) + (P("mp"),) * 6,
        out_specs=(cut, cut, tap, tap, P(None, "mp")) + (P("mp"),) * 6,
        check_vma=False,
    )
```

profile of v0, /device:TPU:0, one launch (start us, length us, event | category | flops | bytes accessed | tf_op | source)
XLA Modules:
  0.0 179.5 jit_solution(14566232852153654563)
XLA Ops:
  0.6 165.4 %forward_and_backward.1 = (bf16[2048,768]{1,0:T(8,128)(2,1)}, bf16[2,2048,384]{2,1,0:T(8,128)(2,1)}, bf16[2,1024,384]{2,1,0:T(8,128)(2,1)}, bf16[5,768,384]{2,1,...) custom-call(bf16[4096,384]{1,0:T(8,128)(2,1)} %bitcast.8, s32[16,1024]{1,0:T(8,128)} %refs_1_.1, ...), custom_call_target="tpu_custom_call" | custom-call | flops 44000002048 | bytes 40000000 | tf_op jit(solution)/shard_map/forward_and_backward/pallas_call | solution.py:1168
  166.0 13.3 %last_pass.1 = (f32[16,256,384]{2,1,0:T(8,128)}, bf16[16,128,384]{2,1,0:T(8,128)(2,1)}, f32[3840,384]{1,0:T(8,128)}, f32[576,768]{1,0:T(8,128)}, f32[384,384]{1,...) custom-call(bf16[16,256,384]{2,1,0:T(8,128)(2,1)} %sig.1, ...), custom_call_target="tpu_custom_call" | custom-call | tf_op jit(solution)/shard_map/last_pass/pallas_call | solution.py:1241
where the time goes:
time: 180 us
  Pallas kernels  179 us (99%)
    pallas_call x1, Pallas kernels, call_main(): pl.pallas_call(functools.partial(main_body, (nb, nm, na, T, S, CH, HC), n...  165 us
    pallas_call x1, Pallas kernels, call_last(): pl.pallas_call(functools.partial(last_body, (CH, total_in)), grid=(steps,...  13.3 us

commit v1 on v0

--- a/solution.py
+++ b/solution.py
@@ -704,8 +704,37 @@
 
     lax.fori_loop(0, PR // 128, make_mid, 0)
 
-    RS = [part("RS", 0, rim), part("RS", rim, rim)]
-    RR = [part("RR", 0, rim), part("RR", rim, rim)]
+    packed = early
+    WIN = 32 * ROWS
+    nrim = WIN if packed else rim
+    RS = [part("RS", 0, nrim), part("RS", rim, nrim)]
+    RR = [part("RR", 0, nrim), part("RR", rim, nrim)]
+
+    def ended(s):
+        before = SEGX[pl.ds(al(BIN0 + (s - 33) * 16, 8), 8), :]
+        after = SEGX[pl.ds(al(BIN0 + s * 16, 8), 8), :]
+        return wide(jnp.where(before != after, 1.0, 0.0), HC // 128).reshape(1, ROWS, HC)
+
+    ended_up, ended_down = ended(S), ended(0)
+
+    def choose(flag, x, y):
+        three = (WIN // ROWS, ROWS, HC)
+        return jnp.where(flag > 0.5, x.reshape(three), y.reshape(three)).reshape(WIN, HC)
+
+    def pack_up(start):
+        at = lambda s: r.F[pl.ds(start + s * ROWS, WIN), :]
+        return choose(ended_up, at(S - 32), at(S - DIL)).astype(BF)
+
+    def pack_down(start):
+        at = lambda s: r.F[pl.ds(start + s * ROWS, WIN), :]
+        return choose(ended_down, at(DIL - 32), at(0)).astype(BF)
+
+    def unpack(flag, ref, v, first):
+        ref[...] = jnp.zeros((rim, HC), F32)
+        a, c = first * ROWS, (first + DIL - 32) * ROWS
+        ref[a : a + WIN, :] = choose(flag, jnp.zeros((WIN, HC), F32), v)
+        ref[c : c + WIN, :] = choose(flag, v, ref[c : c + WIN, :])
+
     p_rims = Rims(RS[1], RR[1], RS[0], RR[0], 2)
     QR = PR // 4
     e0_at, e1_at, do_at, hm_at = spans["E0"][1], spans["GM"][1], spans["DO"][1], spans["HM"][1]
@@ -730,12 +759,12 @@
 
         @pl.when(i == 1)
         def _():
-            RS[0][...] = E0[PR : PR + rim, :].astype(BF)
+            RS[0][...] = pack_up(e0_at + rim) if packed else E0[PR : PR + rim, :].astype(BF)
             p_rims.start_up()
 
         @pl.when(i == 3)
         def _():
-            RS[1][...] = E1[0:rim, :].astype(BF)
+            RS[1][...] = pack_down(e1_at) if packed else E1[0:rim, :].astype(BF)
             p_rims.start_down()
 
         return 0
@@ -748,7 +777,11 @@
 
         @pl.when(has_down)
         def _():
-            low[...] = RR[0][...].astype(F32)
+            v = RR[0][...].astype(F32)
+            if packed:
+                unpack(ended_down, low, v, 1)
+            else:
+                low[...] = v
 
         @pl.when(jnp.logical_not(has_down))
         def _():
@@ -756,7 +789,11 @@
 
         @pl.when(has_up)
         def _():
-            high[...] = RR[1][...].astype(F32)
+            v = RR[1][...].astype(F32)
+            if packed:
+                unpack(ended_up, high, v, 0)
+            else:
+                high[...] = v
 
         @pl.when(jnp.logical_not(has_up))
         def _():
@@ -845,7 +882,12 @@
 
     lax.fori_loop(0, PR // 128, make_gd, 0)
     p_rims.drain()
-    g_rims = Rims(part("GD", PR, rim), RR[1], part("GD", 2 * PR - rim, rim), RR[0], 4)
+    if packed:
+        RS[0][...] = pack_up(e0_at + rim)
+        RS[1][...] = pack_down(e0_at + rim)
+        g_rims = Rims(RS[1], RR[1], RS[0], RR[0], 4)
+    else:
+        g_rims = Rims(part("GD", PR, rim), RR[1], part("GD", 2 * PR - rim, rim), RR[0], 4)
     g_rims.start_up()
     g_rims.start_down()
 
@@ -1180,44 +1222,129 @@
     return dict(zip(outs, res, strict=True))
 
 
-def last_body(dims, sig, da, out, rr, dk0, dk1, pw, stats, gs_ref, out_ref, gw_ref, dk_ref, pw_ref,
-              g0, g1, g2, g3, g4, g5, lanes, lanes2):
+def last_body(dims, sig, da, out, rr, dp, stats, gs, oo, gw, dk, pw, g0, g1, g2, g3, g4, g5,
+              sig_v, da_v, out_v, rr_v, dp_v, st_v, gs_v, oo_v, gw_v, dk_v, pw_v, lanes, ls, ss):
     CH, total_in = dims
     m = lax.axis_index("mp")
-    step = pl.program_id(0)
-    n = da.shape[1]
-    BB = n // ROWS
-    v = da[0].astype(F32)
-    u = out[0].astype(F32)
-    n2 = out.shape[1]
-    B2 = n2 // ROWS
-    for j in range(CH // 128):
-        lanes[j * n : (j + 1) * n, :] = v[:, j * 128 : (j + 1) * 128]
-        lanes2[j * n2 : (j + 1) * n2, :] = u[:, j * 128 : (j + 1) * 128]
-    st = stats[:, pl.ds(al(m * CH, CH), CH)]
+    taps = rr.shape[0]
+    T, S = sig.shape[1], oo.shape[1]
+    HH = g4.shape[0]
+    copy = pltpu.make_async_copy
+
+    def load(src, dst, i):
+        return copy(src, dst, ls.at[i])
+
+    def load_tap(k):
+        return load(rr.at[k], rr_v.at[k], k)
+
+    def load_half(h):
+        rows = pl.ds(h * ROWS, ROWS)
+        return [
+            load(da.at[h], da_v.at[h], taps + 3 * h),
+            load(sig.at[rows], sig_v.at[rows], taps + 3 * h + 1),
+            load(out.at[h], out_v.at[h], taps + 3 * h + 2),
+        ]
+
+    ld_st = load(stats, st_v, taps + 6)
+    ld_dp = load(dp, dp_v, taps + 7)
+    ld_st.start()
+    for k in range(taps):
+        load_tap(k).start()
+    for h in range(2):
+        for c in load_half(h):
+            c.start()
+    ld_dp.start()
+
+    def store_tap(k):
+        return copy(gw_v.at[k], gw.at[k], ss.at[k])
+
+    def tap(k, _):
+        load_tap(k).wait()
+
+        def part(i, _):
+            at = pl.ds(al(i * 96, 96), 96)
+            gw_v[k, at, :] = rr_v[k, at, :].astype(F32)
+            return 0
+
+        lax.fori_loop(0, rr.shape[1] // 96, part, 0)
+        store_tap(k).start()
+        return 0
+
+    lax.fori_loop(0, taps, tap, 0)
+    ld_st.wait()
+    st = st_v[:, pl.ds(al(m * CH, CH), CH)]
     mu, inv, gain, gg, gb = [st[i : i + 1] for i in (0, 1, 2, 4, 5)]
     scale = gain * inv
     mg, mb = gg / total_in, gb / total_in
-    for row in range(ROWS):
+    BB = 64
+    n = BB * ROWS
+
+    def store_gs(h, c):
+        at = (pl.ds(h * ROWS, ROWS), pl.ds(al(c * BB, BB), BB))
+        return copy(gs_v.at[at], gs.at[at], ss.at[taps + h * (T // BB) + c])
+
+    def store_oo(h):
+        at = pl.ds(h * ROWS, ROWS)
+        return copy(oo_v.at[at], oo.at[at], ss.at[taps + 2 * (T // BB) + h])
+
+    def fill(v):
         for j in range(CH // 128):
-            c = slice(j * 128, (j + 1) * 128)
-            d = lanes[pl.ds(j * n + row, BB, stride=ROWS), :]
-            xhat = (sig[row, :, c].astype(F32) - mu[:, c]) * inv[:, c]
-            gs_ref[row, :, c] = scale[:, c] * (d - mb[:, c] - xhat * mg[:, c])
-            out_ref[row, :, c] = lanes2[pl.ds(j * n2 + row, B2, stride=ROWS), :].astype(BF)
-    gw_ref[...] = rr[...].astype(F32)
-    dk_ref[...] = jnp.concatenate([dk0[...].astype(F32), dk1[...].astype(F32)], axis=1)
-    pw_ref[...] = pw[...].astype(F32)
-
-    @pl.when(step == 0)
-    def _():
-        for ref, i in ((g0, 4), (g1, 5), (g2, 6), (g3, 7)):
-            ref[...] = st[i : i + 1].reshape(CH)
-        HH = g4.shape[0]
-        hid = stats[8:10, : 2 * HH]
-        hid = jnp.where(m == 0, hid[:, :HH], hid[:, HH:])
-        g4[...] = hid[0:1].reshape(HH)
-        g5[...] = hid[1:2].reshape(HH)
+            lanes[j * n : (j + 1) * n, :] = v[:, j * 128 : (j + 1) * 128].astype(F32)
+
+    def half(h, _):
+        for c in load_half(h):
+            c.wait()
+
+        def block(c, _):
+            fill(da_v[h, pl.ds(al(c * n, n), n), :])
+            bins = pl.ds(al(c * BB, BB), BB)
+            for row in range(ROWS):
+                for j in range(CH // 128):
+                    l = slice(j * 128, (j + 1) * 128)
+                    d = lanes[pl.ds(j * n + row, BB, stride=ROWS), :]
+                    xhat = (sig_v[h * ROWS + row, bins, l].astype(F32) - mu[:, l]) * inv[:, l]
+                    gs_v[h * ROWS + row, bins, l] = scale[:, l] * (d - mb[:, l] - xhat * mg[:, l])
+            store_gs(h, c).start()
+            return 0
+
+        lax.fori_loop(0, T // BB, block, 0)
+
+        def block2(c, _):
+            fill(out_v[h, pl.ds(al(c * n, n), n), :])
+            bins = pl.ds(al(c * BB, BB), BB)
+            for row in range(ROWS):
+                for j in range(CH // 128):
+                    oo_v[h * ROWS + row, bins, j * 128 : (j + 1) * 128] = lanes[pl.ds(j * n + row, BB, stride=ROWS), :].astype(BF)
+            return 0
+
+        lax.fori_loop(0, S // BB, block2, 0)
+        store_oo(h).start()
+        return 0
+
+    lax.fori_loop(0, 2, half, 0)
+    ld_dp.wait()
+    for k, at in enumerate((0, 6, 2)):
+        for h in range(2):
+            dk_v[k * HH : (k + 1) * HH, h * CH : (h + 1) * CH] = dp_v[(at + h) * HH : (at + h + 1) * HH, :].astype(F32)
+    pw_v[...] = dp_v[4 * HH : 6 * HH, :].astype(F32)
+    st_dk = copy(dk_v, dk, ss.at[taps + 2 * (T // BB) + 2])
+    st_pw = copy(pw_v, pw, ss.at[taps + 2 * (T // BB) + 3])
+    st_dk.start()
+    st_pw.start()
+    for ref, i in ((g0, 4), (g1, 5), (g2, 6), (g3, 7)):
+        ref[...] = st[i : i + 1].reshape(CH)
+    hid = st_v[8:10, : 2 * HH]
+    hid = jnp.where(m == 0, hid[:, :HH], hid[:, HH:])
+    g4[...] = hid[0:1].reshape(HH)
+    g5[...] = hid[1:2].reshape(HH)
+    for k in range(taps):
+        store_tap(k).wait()
+    for h in range(2):
+        for c in range(T // BB):
+            store_gs(h, c).wait()
+        store_oo(h).wait()
+    st_dk.wait()
+    st_pw.wait()
 
 
 def call_last(axes, sig, o):
@@ -1227,55 +1354,25 @@
     C = 2 * CH
     HC = CH
     HH = HC // 2
-    NC = 4
-    steps = 2 * NC
+    rr = o["oR"]
+    total_in = float(rows * T * nb * na)
     sd = jax.ShapeDtypeStruct
-    total_in = float(rows * T * nb * na)
-    rr = o["oR"].reshape(-1, CH)
-    dp = o["oDP"]
-    flat = lambda n, w: pl.BlockSpec((n, w), lambda i: (i, 0))
-    whole1 = pl.BlockSpec(memory_space=pltpu.VMEM)
-    nr, npw, nd = rr.shape[0] // steps, HC // steps, HH
-    tap_of = lambda i: jnp.minimum(i // 2, 2)
-    base = lambda i: jnp.where(tap_of(i) == 1, 6, tap_of(i))
+    V = pltpu.VMEM
+    anyspec = pl.BlockSpec(memory_space=pl.ANY)
+    vmem = pl.BlockSpec(memory_space=pltpu.VMEM)
+    inputs = (sig, o["oDA"], o["oOUT"], rr, o["oDP"], o["oST"])
+    big = [sd((rows, T, CH), F32), sd((rows, S, CH), BF), sd(rr.shape, F32), sd((3 * HH, C), F32), sd((HC, CH), F32)]
     return pl.pallas_call(
         functools.partial(last_body, (CH, total_in)),
-        grid=(steps,),
-        out_shape=[
-            sd((rows, T, CH), F32),
-            sd((rows, S, CH), BF),
-            sd(rr.shape, F32),
-            sd((3 * HH, C), F32),
-            sd((HC, CH), F32),
-            *[sd((CH,), F32)] * 4,
-            *[sd((HH,), F32)] * 2,
-        ],
-        in_specs=[
-            pl.BlockSpec((ROWS, T // NC, CH), lambda i: (i // NC, i % NC, 0)),
-            pl.BlockSpec((1, T * ROWS // NC, CH), lambda i: (i // NC, i % NC, 0)),
-            pl.BlockSpec((1, S * ROWS // NC, CH), lambda i: (i // NC, i % NC, 0)),
-            flat(nr, CH),
-            pl.BlockSpec((nd, CH), lambda i: (base(i), 0)),
-            pl.BlockSpec((nd, CH), lambda i: (base(i) + 1, 0)),
-            pl.BlockSpec((npw, CH), lambda i: (4 * HH // npw + i, 0)),
-            pl.BlockSpec((16, C), lambda i: (0, 0)),
-        ],
-        out_specs=[
-            pl.BlockSpec((ROWS, T // NC, CH), lambda i: (i // NC, i % NC, 0)),
-            pl.BlockSpec((ROWS, S // NC, CH), lambda i: (i // NC, i % NC, 0)),
-            flat(nr, CH),
-            pl.BlockSpec((nd, C), lambda i: (tap_of(i), 0)),
-            flat(npw, CH),
-            *[pl.BlockSpec((CH,), lambda i: (0,))] * 4,
-            *[pl.BlockSpec((HH,), lambda i: (0,))] * 2,
-        ],
-        scratch_shapes=[
-            pltpu.VMEM((CH // 128 * T * ROWS // NC, 128), F32),
-            pltpu.VMEM((CH // 128 * S * ROWS // NC, 128), F32),
-        ],
+        out_shape=big + [sd((CH,), F32)] * 4 + [sd((HH,), F32)] * 2,
+        in_specs=[anyspec] * len(inputs),
+        out_specs=[anyspec] * len(big) + [vmem] * 6,
+        scratch_shapes=[V(x.shape, x.dtype) for x in inputs]
+        + [V(x.shape, x.dtype) for x in big]
+        + [V((CH // 128 * 64 * ROWS, 128), F32), pltpu.SemaphoreType.DMA((rr.shape[0] + 8,)), pltpu.SemaphoreType.DMA((rr.shape[0] + T // 32 + 4,))],
         compiler_params=pltpu.CompilerParams(vmem_limit_bytes=VMEM_BYTES),
         name="last_pass",
-    )(sig, o["oDA"], o["oOUT"], rr, dp, dp, dp, o["oST"])
+    )(*inputs)
 
 
 def on_device(axes, signal, seg, cotangent, conv_wide, taps, pointwise, *vectors):

time: 180 us -> 171 us (0.950)
  Pallas kernels: 179 us -> 170 us
    pallas_call x1, Pallas kernels: 165 us -> 159 us  [call_main(): pl.pallas_call(functools.partial(main_body, (nb, nm, na, T, S, CH, HC), n...]
    pallas_call x1, Pallas kernels: 13.3 us -> 10.6 us  [call_last(): pl.pallas_call(functools.partial(last_body, (CH, total_in)), out_shape=bi...]
where the time goes in v1:
time: 171 us
  Pallas kernels  170 us (99%)
    pallas_call x1, Pallas kernels, call_main(): pl.pallas_call(functools.partial(main_body, (nb, nm, na, T, S, CH, HC), n...  159 us
    pallas_call x1, Pallas kernels, call_last(): pl.pallas_call(functools.partial(last_body, (CH, total_in)), out_shape=bi...  10.6 us

profile of v1, /device:TPU:0, one launch (start us, length us, event | category | flops | bytes accessed | tf_op | source)
XLA Modules:
  0.0 170.7 jit_solution(16081514399405219950)
XLA Ops:
  0.6 159.4 %forward_and_backward.1 = (bf16[2048,768]{1,0:T(8,128)(2,1)}, bf16[2,2048,384]{2,1,0:T(8,128)(2,1)}, bf16[2,1024,384]{2,1,0:T(8,128)(2,1)}, bf16[5,768,384]{2,1,...) custom-call(bf16[4096,384]{1,0:T(8,128)(2,1)} %bitcast.6, s32[16,1024]{1,0:T(8,128)} %refs_1_.1, ...), custom_call_target="tpu_custom_call" | custom-call | flops 44000002048 | bytes 40000000 | tf_op jit(solution)/shard_map/forward_and_backward/pallas_call | solution.py:1210
  160.0 10.6 %last_pass.1 = (f32[16,256,384]{2,1,0:T(8,128)}, bf16[16,128,384]{2,1,0:T(8,128)(2,1)}, f32[5,768,384]{2,1,0:T(8,128)}, f32[576,768]{1,0:T(8,128)}, f32[384,384]...) custom-call(bf16[16,256,384]{2,1,0:T(8,128)(2,1)} %sig.1, ...), custom_call_target="tpu_custom_call" | custom-call | tf_op jit(solution)/shard_map/last_pass/pallas_call | solution.py:1365

commit v2 on v1

--- a/solution.py
+++ b/solution.py
@@ -82,17 +82,20 @@
 
     def start(self, value):
         self.buf[self.me] = value
+        own = self.buf.at[self.me]
         for q in self.others:
-            remote(self.buf.at[self.me], self.buf.at[self.me], self.ss.at[q], self.rs.at[self.me], self.dev_of(q)).start()
+            remote(own, own, self.ss, self.rs, self.dev_of(q)).start()
+
+    def all_others(self):
+        ref = self.buf.at[pl.ds(0, self.n - 1)]
+        return remote(ref, ref, self.ss, self.rs, self.dev_of(self.others[0]))
 
     def wait(self):
-        for q in self.others:
-            remote(self.buf.at[q], self.buf.at[q], self.ss.at[q], self.rs.at[q], self.dev_of(q)).wait_recv()
+        self.all_others().wait_recv()
         return [self.buf[i] for i in range(self.n)]
 
     def drain(self):
-        for q in self.others:
-            remote(self.buf.at[self.me], self.buf.at[self.me], self.ss.at[q], self.rs.at[q], self.dev_of(q)).wait_send()
+        self.all_others().wait_send()
 
 
 def merged(parts, count):
@@ -108,10 +111,8 @@
     return jnp.sum(x, axis=0, keepdims=True)
 
 
-def greet(place):
+def greet(devices):
     barrier = pltpu.get_barrier_semaphore()
-    devices = [place.in_layer(q) for q in place.others(place.q, place.layer)]
-    devices += [place.in_bins(b) for b in place.others(place.b, place.nb)]
     for d in devices:
         pl.semaphore_signal(barrier, inc=1, device_id=d, device_id_type=MESH)
     pl.semaphore_wait(barrier, len(devices))
@@ -126,33 +127,33 @@
     ("bm2", [18]),
     ("tap0", [19, 15, 16, 17]),
     ("tap1", [18, 0, 2]),
-    ("tap2", [1]),
-    ("tap3", [15, 16, 17, 4]),
+    ("tap2", [1, 15, 16]),
+    ("tap3", [17, 4]),
     ("tap4", [3, 5]),
     ("tap5", [18, 1, 6, 8]),
     ("tap6", [19, 0, 15, 7]),
-    ("tap7", [16, 2, 3, 10]),
-    ("tap8", [17, 4, 5, 9, 11]),
-    ("tap9", [1, 0, 15, 12, 14]),
-    ("taps", [6, 7, 16, 13]),
-    ("tile0", [2, 8, 4, 17]),
-    ("tile1", [19]),
-    ("tile2", [1, 9, 3, 0]),
-    ("tile3", [11]),
-    ("tile4", [10, 6, 2, 5]),
-    ("tile5", [16, 4, 15]),
-    ("tile6", [1, 13, 12]),
-    ("tile7", [3, 8]),
-    ("tile8", [0, 14, 6]),
-    ("tile9", [7, 2, 19]),
-    ("tile10", [17, 5, 10, 9, 4]),
-    ("tile11", [11]),
-    ("tile12", [3, 15, 8, 12, 16]),
-    ("tile13", [6, 0]),
-    ("tile14", [1, 7, 14, 13, 5, 2]),
-    ("tile15", [10, 3]),
-    ("end0", [9, 17, 11, 4, 0, 8, 6, 5, 12, 7, 1, 2, 14]),
-    ("end1", [13, 3, 4, 10, 8, 9, 6, 11, 5, 7, 12, 10, 14, 8, 13, 9, 11, 7, 12, 10, 14, 13, 9, 12, 11, 14, 13]),
+    ("tap7", [16, 2, 3, 17, 10]),
+    ("tap8", [4, 5, 1, 9, 11, 0]),
+    ("tap9", [15, 6, 12, 14, 7]),
+    ("taps", [16, 2, 13, 17]),
+    ("tile0", [8, 4, 1, 19]),
+    ("tile1", [0, 9, 3]),
+    ("tile2", [2, 11]),
+    ("tile3", [10]),
+    ("tile4", [6, 5, 4, 16, 15, 1]),
+    ("tile5", []),
+    ("tile6", [0, 13, 12, 3, 8]),
+    ("tile7", [2, 14]),
+    ("tile8", [7, 6, 19, 17, 5]),
+    ("tile9", [10, 9, 4]),
+    ("tile10", [11, 3, 15, 8]),
+    ("tile11", [0]),
+    ("tile12", [16, 7, 12, 1, 6, 2, 13]),
+    ("tile13", [5, 14]),
+    ("tile14", [3, 10, 9]),
+    ("tile15", [17, 0]),
+    ("end0", [11, 4, 8, 2, 7, 1, 5, 12, 6, 13, 4, 14]),
+    ("end1", [3, 7, 10, 8, 9, 6, 11, 5, 12, 13, 7, 8, 14, 10, 9, 12, 11, 13, 14, 10, 9, 12, 11, 14, 13]),
 )
 
 
@@ -170,6 +171,7 @@
     total_mid = float(PR * nb * nm * na)
     LANES = r.LANES
     RT = LANES.shape[0] // (C // 128)
+    early = nb == 4
 
     def part(name, at=0, n=None):
         pool, start, rows = spans[name]
@@ -216,7 +218,14 @@
         PAR[m, i : i + 1, :] = vectors[i][...].reshape(1, CH)
     for i in range(4, 6):
         PAR[m, i : i + 1, 0:HH] = vectors[i][...].reshape(1, HH)
-    greet(place)
+    if early:
+        chips, chip = nb * na, b * na + a
+        first = (m, nm, lambda q: (b, q, a))
+        second = (chip, chips, lambda q: (q // na, m, lax.rem(q, na)))
+    else:
+        first = (place.q, place.layer, place.in_layer)
+        second = (b, nb, place.in_bins)
+    greet([g[2](q) for g in (first, second) for q in place.others(*g[:2])])
     x_sig = cross(sig.at[theirs], raw_mine, 0)
     x_par = cross(PAR.at[m], PAR.at[m], 1)
     x_w = [cross(r.wide.at[k], weight(k), 2 + k) for k in range(TAPS)]
@@ -228,26 +237,31 @@
         c.start()
 
     def exchange(i, name):
+        one, two = (second, first) if early and i == 0 else (first, second)
         return (
-            Exchange(getattr(r, name + "A"), place.q, place.layer, place.in_layer, r.as_.at[i], r.ar_.at[i], place.others(place.q, place.layer)),
-            Exchange(getattr(r, name + "B"), b, nb, place.in_bins, r.bs_.at[i], r.br_.at[i], place.others(b, nb)),
+            Exchange(getattr(r, name + "A"), *one, r.as_.at[i], r.ar_.at[i], place.others(*one[:2])),
+            Exchange(getattr(r, name + "B"), *two, r.bs_.at[i], r.br_.at[i], place.others(*two[:2])),
         )
 
+    def begin_stats(ex, mean, squares, count):
+        ex[0].start(jnp.concatenate([mean, squares], axis=0))
+        ex[1].start(jnp.concatenate(merged(ex[0].wait(), count), axis=0))
+
     def finish_stats(ex, count):
-        mean, squares = merged(ex[0].wait(), count)
-        ex[1].start(jnp.concatenate([mean, squares], axis=0))
-        return merged(ex[1].wait(), count * place.layer)
-
-    def finish_sums(ex, between=lambda: None):
+        return merged(ex[1].wait(), count * first[1])
+
+    def begin_sums(ex, one, two):
+        ex[0].start(jnp.concatenate([one, two], axis=0))
         ex[1].start(functools.reduce(jnp.add, ex[0].wait()))
-        between()
+
+    def finish_sums(ex):
         return functools.reduce(jnp.add, ex[1].wait())
 
     ex_in, ex_mid, ex_hid, ex_bh, ex_bm, ex_bi = exchanges = [
         exchange(i, n) for i, n in enumerate(["XI", "XM", "XH", "XG", "XD", "XS"])
     ]
 
-    ps, pr, zs, zr = r.ps, r.pr, r.zs, r.zr
+    ps, pr, zr = r.ps, r.pr, r.zr
     N = r.N
     INNER = 4
     outer = nb // INNER
@@ -255,7 +269,6 @@
     base = b - inner
     bits = (lax.rem(a, 2), a // 2)
     flip = ((b, m, a + 1 - 2 * bits[0]), (b, m, lax.rem(a + 2, 4)))
-    early = outer == 1
     PSLOTS = spans["PS"][2] // C
 
     class Piece:
@@ -289,7 +302,7 @@
             N[pl.ds(al(start + at, 16), n), self.lanes] = v.astype(BF)
 
         def describe(self, make, i, dev):
-            return lambda: remote(*make(), ps.at[self.p, i], pr.at[self.p, i], dev)
+            return lambda: remote(*make(), ps.at[self.p], pr.at[self.p, i - 2], dev)
 
         def moves(self):
             F, R = self.F, self.R
@@ -308,23 +321,17 @@
                 src, dst = self.rows(self.R, self.k2 + j * self.SMALL, self.SMALL), self.rows(self.ZB, inner * self.SMALL, self.SMALL)
             else:
                 src = dst = self.rows(self.F, self.k2 + inner * self.SMALL, self.SMALL)
-            return remote(src, dst, zs.at[self.p, which, j], zr.at[self.p, which, inner], (base + j, m, a))
+            return remote(src, dst, ps.at[self.p], zr.at[self.p, which], (base + j, m, a))
 
         def gather(self, which):
-            for i in range(1, INNER):
-                j = lax.rem(inner + i, INNER)
-                if self.full:
-                    ref = self.rows(self.ZB, j * self.QUART, self.QUART)
-                else:
-                    ref = self.rows(self.ZB, j * self.SMALL, self.SMALL) if which == 0 else self.rows(self.F, self.k2 + j * self.SMALL, self.SMALL)
-                remote(ref, ref, zs.at[self.p, which, j], zr.at[self.p, which, j], (base + j, m, a)).wait_recv()
+            n = (INNER - 1) * (self.QUART if self.full else self.SMALL)
+            ref = self.rows(self.ZB, 0, n) if which == 0 else self.rows(self.F, self.k2, n)
+            remote(ref, ref, ps.at[self.p], zr.at[self.p, which], (base + lax.rem(inner + 1, INNER), m, a)).wait_recv()
 
         def drain(self):
-            for i in (2, 3, 4, 5):
-                self.moves()[i]().wait_send()
-            for which in range(1 if self.full else 2):
-                for i in range(1, INNER):
-                    self.toward(which, i).wait_send()
+            n = self.n + self.n // 2 + (INNER - 1) * (self.QUART if self.full else 2 * self.SMALL)
+            ref = N.at[pl.ds(0, n), self.lanes]
+            remote(ref, ref, ps.at[self.p], pr.at[self.p, 0], self.n1).wait_send()
             if outer > 1:
                 for i in range(1, outer):
                     self.outward(i).wait_send()
@@ -435,8 +442,8 @@
             which = [p for p in which if p < len(pieces) and not (p == late and name in ("bh", "center", "center2"))]
         plan[name] = [(p, left[p].pop(0)) for p in which if left[p]]
     while any(left):
-        first = max(len(x) for x in left)
-        plan["end1"] += [(p, x.pop(0)) for p, x in enumerate(left) if len(x) == first]
+        most = max(len(x) for x in left)
+        plan["end1"] += [(p, x.pop(0)) for p, x in enumerate(left) if len(x) == most]
 
     def pump(where):
         for p, ph in plan[where]:
@@ -518,12 +525,15 @@
 
     la = ex_in[0].wait()
     n_own = float(2 * HR)
-    lo = merged(la[0:na], n_own)
-    hi = merged(la[na : 2 * na], n_own)
-    ex_in[1].start(
-        jnp.concatenate([jnp.concatenate([lo[0], hi[0]], axis=1), jnp.concatenate([lo[1], hi[1]], axis=1)], axis=0)
-    )
-    mu_in, sq = merged(ex_in[1].wait(), n_own * na)
+    both = lambda x, y: jnp.concatenate([jnp.concatenate([x[i], y[i]], axis=1) for i in range(2)], axis=0)
+    if early:
+        ex_in[1].start(jnp.concatenate(merged(la, n_own), axis=0))
+        lb = ex_in[1].wait()
+        v = both((lb[0][0:1], lb[0][1:2]), (lb[1][0:1], lb[1][1:2]))
+        mu_in, sq = v[0:1], v[1:2]
+    else:
+        ex_in[1].start(both(merged(la[0:na], n_own), merged(la[na : 2 * na], n_own)))
+        mu_in, sq = merged(ex_in[1].wait(), n_own * na)
     inv_in = lax.rsqrt(sq / total_in + EPSILON)
     gain_in, shift_in = vec(0), vec(1)
     scale_in = gain_in * inv_in
@@ -663,7 +673,7 @@
         return acc + jnp.sum(v * v, axis=0)
 
     acc = lax.fori_loop(0, PR // 128, m2_mid, jnp.zeros((8, C), F32))
-    ex_mid[0].start(jnp.concatenate([mean, row_sum(acc)], axis=0))
+    begin_stats(ex_mid, mean, row_sum(acc), float(PR))
 
     ld_cot.wait()
     x_cot.wait_recv()
@@ -736,7 +746,7 @@
         ref[c : c + WIN, :] = choose(flag, v, ref[c : c + WIN, :])
 
     p_rims = Rims(RS[1], RR[1], RS[0], RR[0], 2)
-    QR = PR // 4
+    QR = PR // 2
     e0_at, e1_at, do_at, hm_at = spans["E0"][1], spans["GM"][1], spans["DO"][1], spans["HM"][1]
 
     def pick(i, table):
@@ -745,31 +755,31 @@
             v = jnp.where(i == n, table[n], v)
         return v
 
-    quarter = (3, 2, 0, 1, 0, 1, 2, 3, 0, 1, 2, 3)
-    taps_of = (0, 0, 2, 2, 0, 0, 2, 2, 1, 1, 1, 1)
-    starts = [{0: e0_at + rim, 1: do_at, 2: e1_at}[k] + q * QR for k, q in zip(taps_of, quarter)]
+    halves_of = (1, 0, 0, 1, 0, 1)
+    taps_of = (0, 2, 0, 2, 1, 1)
+    starts = [{0: e0_at + rim, 1: do_at, 2: e1_at}[k] + q * QR for k, q in zip(taps_of, halves_of)]
 
     def product(i, _):
         v = dot(
-            r.M[pl.ds(al(hm_at + pick(i, quarter) * QR, 16), QR), :],
+            r.M[pl.ds(al(hm_at + pick(i, halves_of) * QR, 16), QR), :],
             r.M[pl.ds(al(dt0 + pick(i, taps_of) * HC, 16), HC), :],
             1, 1,
         )
         r.F[pl.ds(al(pick(i, starts), 8), QR), :] = v
 
-        @pl.when(i == 1)
+        @pl.when(i == 0)
         def _():
             RS[0][...] = pack_up(e0_at + rim) if packed else E0[PR : PR + rim, :].astype(BF)
             p_rims.start_up()
 
-        @pl.when(i == 3)
+        @pl.when(i == 1)
         def _():
             RS[1][...] = pack_down(e1_at) if packed else E1[0:rim, :].astype(BF)
             p_rims.start_down()
 
         return 0
 
-    lax.fori_loop(0, len(quarter), product, 0)
+    lax.fori_loop(0, len(halves_of), product, 0)
 
     def take_rims(rims, low, high):
         rims.wait_from_down()
@@ -823,7 +833,25 @@
         return acc + jnp.sum(v * v, axis=0)
 
     acc = lax.fori_loop(0, PR // 128, m2_hid, jnp.zeros((8, HC), F32))
-    ex_hid[0].start(jnp.concatenate([mean, row_sum(acc)], axis=0))
+    begin_stats(ex_hid, mean, row_sum(acc), float(PR))
+    SL = [part("RAW", 0, PR), part("RAW", PR, PR)]
+
+    def make_slope(i, _):
+        at = pl.ds(al(i * 64, 64), 64)
+        _, slope = gelu_both((POOL[at, :] - mu_mid) * scale_mid + shift_mid)
+        SL[0][at, :] = slope[:, :CH].astype(BF)
+        SL[1][at, :] = slope[:, CH:].astype(BF)
+        return 0
+
+    lax.fori_loop(0, PR // 64, make_slope, 0)
+
+
+    def pool_weights(i, _):
+        at = pl.ds(al(i * 64, 64), 64)
+        DIFF[at, :] = 0.5 + 0.5 * jnp.tanh(0.5 * DIFF[at, :])
+        return 0
+
+    lax.fori_loop(0, PR // 64, pool_weights, 0)
     mu_hid, sq = finish_stats(ex_hid, float(PR))
     inv_hid = lax.rsqrt(sq / total_mid + EPSILON)
     gain_hid, shift_hid = hvec(4), hvec(5)
@@ -844,7 +872,7 @@
 
     zero = jnp.zeros((8, HC), F32)
     sg, sb = lax.fori_loop(0, PR // 128, make_top, (zero, zero))
-    ex_bh[0].start(jnp.concatenate([row_sum(sg), row_sum(sb)], axis=0))
+    begin_sums(ex_bh, row_sum(sg), row_sum(sb))
 
     OB = 256
 
@@ -866,7 +894,9 @@
     N[dps_at + C : dps_at + C + HC, :] = jnp.where(m == 0, gp[:, CH:], gp[:, :CH]).astype(BF)
     share_pw.copy().start()
 
-    v = finish_sums(ex_bh, lambda: (share_pw.sum(), pump("bh")))
+    share_pw.sum()
+    pump("bh")
+    v = finish_sums(ex_bh)
     ST[8:10, 0:HC] = v
     ST[8:10, HC:] = jnp.zeros((2, C - HC), F32)
     scale = gain_hid * inv_hid
@@ -892,18 +922,17 @@
     g_rims.start_down()
 
 
-    def to_gm(make, add):
-        def body(i, _):
-            at = pl.ds(al(i * QR, QR), QR)
-            v = make(at)
-            for h in range(2):
-                u = v[:, h * CH : (h + 1) * CH]
-                GML[h][at, :] = GML[h][at, :] + u if add else u
-            return 0
-
-        lax.fori_loop(0, 4, body, 0)
-
-    to_gm(lambda at: dot(GD[1][at, :], dt(1), 1, 0), False)
+    def to_gm(i, v, add):
+        at = pl.ds(al(i * QR, QR), QR)
+        for h in range(2):
+            u = v[:, h * CH : (h + 1) * CH]
+            GML[h][at, :] = GML[h][at, :] + u if add else u
+
+    def mid_center(i, _):
+        to_gm(i, dot(GD[1][pl.ds(al(i * QR, QR), QR), :], dt(1), 1, 0), False)
+        return 0
+
+    lax.fori_loop(0, 2, mid_center, 0)
     gd_at = spans["GD"][1]
 
     def dil_grad(k, to):
@@ -920,17 +949,27 @@
     pump("center")
     share_mid.sum()
     pump("center2")
+    gd_of = [spans["GD"][1], spans["GD"][1] + 2 * PR]
+
+    def mid_side(by, i):
+        g_at = gd_of[0 if by > 0 else 1]
+
+        def body(j, _):
+            n = i * (QR // 128) + j
+            v = same(n, by) * E0[pl.ds(al(n * 128 + rim + by * 8, 8), 128), :]
+            N[pl.ds(al(g_at + n * 128, 16), 128), :] = v.astype(BF)
+            return 0
+
+        lax.fori_loop(0, QR // 128, body, 0)
+        g = N[pl.ds(al(g_at + i * QR, 16), QR), :]
+        to_gm(i, dot(g, dt(0 if by > 0 else 2), 1, 0), True)
+
+    mid_side(DIL, 0)
+    mid_side(-DIL, 1)
     take_rims(g_rims, part("E0", 0, rim), part("E0", PR + rim, rim))
     pump("rims")
-
-    def mask_gd(i, _):
-        at = pl.ds(al(i * 128, 128), 128)
-        GD[0][at, :] = (same(i, DIL) * E0[pl.ds(al(i * 128 + rim + DIL * 8, 8), 128), :]).astype(BF)
-        GD[2][at, :] = (same(i, -DIL) * E0[pl.ds(al(i * 128 + rim - DIL * 8, 8), 128), :]).astype(BF)
-        return 0
-
-    lax.fori_loop(0, PR // 128, mask_gd, 0)
-    to_gm(lambda at: dot(GD[0][at, :], dt(0), 1, 0) + dot(GD[2][at, :], dt(2), 1, 0), True)
+    mid_side(DIL, 1)
+    mid_side(-DIL, 0)
 
     def gm(at):
         return jnp.concatenate([GML[0][at, :], GML[1][at, :]], axis=1)
@@ -938,8 +977,7 @@
     def make_dmid(i, s):
         at = pl.ds(al(i * 64, 64), 64)
         xhat = (POOL[at, :] - mu_mid) * inv_mid
-        _, slope = gelu_both(xhat * gain_mid + shift_mid)
-        da = slope * gm(at)
+        da = jnp.concatenate([SL[0][at, :], SL[1][at, :]], axis=1).astype(F32) * gm(at)
         GML[0][at, :] = da[:, :CH]
         GML[1][at, :] = da[:, CH:]
         return (
@@ -953,11 +991,13 @@
     o_own.wait()
     o_cross.wait_send()
     keep_x.wait()
-    ex_bm[0].start(jnp.concatenate([row_sum(sg), row_sum(sb)], axis=0))
+    begin_sums(ex_bm, row_sum(sg), row_sum(sb))
 
     lax.fori_loop(0, 2, lambda i, _: (dil_grad(2 * i, i * CH), 0)[1], 0)
     share_rest.copy().start()
-    v = finish_sums(ex_bm, lambda: (share_rest.sum(), pump("bm")))
+    share_rest.sum()
+    pump("bm")
+    v = finish_sums(ex_bm)
     ST[6:8, :] = v
     mg, mb = v[0:1] / total_mid, v[1:2] / total_mid
     pump("bm2")
@@ -967,12 +1007,8 @@
         at = pl.ds(al(i * 64, 64), 64)
         xhat = (POOL[at, :] - mu_mid) * inv_mid
         g = CT[at, :].astype(F32) + scale_mid * (gm(at) - mb - xhat * mg)
-        d = DIFF[at, :]
-        e = jnp.exp(-jnp.abs(d))
-        big = 1.0 / (1.0 + e)
-        small = e * big
-        g0 = g * jnp.where(d >= 0, big, small)
-        g1 = g * jnp.where(d >= 0, small, big)
+        g0 = g * DIFF[at, :]
+        g1 = g - g0
         v = jnp.stack([g0.reshape(8, 8, C), g1.reshape(8, 8, C)], axis=1).reshape(128, C)
         GC0[pl.ds(al(i * 128 + 16, 16), 128), :] = v.astype(BF)
         GC1[pl.ds(al(i * 128, 128), 128), :] = jnp.concatenate([last, v[:120]], axis=0).astype(BF)
@@ -1086,15 +1122,14 @@
         return s
 
     s = lax.fori_loop(0, HR // RB, tile, (zero, zero))
-    ex_bi[0].start(jnp.concatenate([row_sum(s[0]), row_sum(s[1])], axis=0))
+    begin_sums(ex_bi, row_sum(s[0]), row_sum(s[1]))
     d_own = local(raw_mine, r.oDA.at[m], 12)
     d_own.start()
     d_cross = cross(r.N.at[pl.ds(al(spans["RAW"][1] + other * HR, 16), HR)], r.oDA.at[m], 13)
     d_cross.start()
     pump("end0")
-    ex_bi[1].start(functools.reduce(jnp.add, ex_bi[0].wait()))
     pump("end1")
-    ST[4:6, :] = functools.reduce(jnp.add, ex_bi[1].wait())
+    ST[4:6, :] = finish_sums(ex_bi)
     ST[3:4, :] = jnp.zeros((1, C), F32)
     ST[10:16, :] = jnp.zeros((6, C), F32)
     o_st = local(ST, r.oST, 14)
@@ -1183,21 +1218,24 @@
         SUM=V((8, C), F32),
         POOL=V((PR, C), F32),
         DIFF=V((PR, C), F32),
-        XIA=V((NA, 2, CH), F32), XIB=V((nb, 2, C), F32),
-        XMA=V((NA, 2, C), F32), XMB=V((nb, 2, C), F32),
-        XHA=V((NA, 2, HC), F32), XHB=V((nb, 2, HC), F32),
-        XGA=V((NA, 2, HC), F32), XGB=V((nb, 2, HC), F32),
-        XDA=V((NA, 2, C), F32), XDB=V((nb, 2, C), F32),
-        XSA=V((NA, 2, C), F32), XSB=V((nb, 2, C), F32),
         lsem=DMA((15 + NP,)),
         shs=DMA((13,)), shr=DMA((13,)),
         csem_s=DMA((14,)), csem_r=DMA((14,)),
-        as_=DMA((6, NA)), ar_=DMA((6, NA)),
-        bs_=DMA((6, nb)), br_=DMA((6, nb)),
+        as_=DMA((6,)), ar_=DMA((6,)),
+        bs_=DMA((6,)), br_=DMA((6,)),
         hs=DMA((8,)), hr=DMA((8,)),
-        ps=DMA((NP, 6)), pr=DMA((NP, 6)),
-        zs=DMA((NP, 2, 4)), zr=DMA((NP, 2, 4)),
+        ps=DMA((NP,)), pr=DMA((NP, 4)),
+        zr=DMA((NP, 2)),
     )
+    for i, (name, width) in enumerate([("XI", C), ("XM", C), ("XH", HC), ("XG", HC), ("XD", C), ("XS", C)]):
+        if early:
+            sizes_ab = (nb * na, nm) if i == 0 else (nm, nb * na)
+            widths = (CH, CH) if i == 0 else (width, width)
+        else:
+            sizes_ab = (NA, nb)
+            widths = (CH if i == 0 else width, width)
+        for x, n, lanes in zip("AB", sizes_ab, widths):
+            scratch[name + x] = V((n, 2, lanes), F32)
     outer = nb // 4
     if outer > 1:
         scratch.update(os_=DMA((NP, outer)), or_=DMA((NP, outer)))

time: 171 us -> 159 us (0.930)
  Pallas kernels: 170 us -> 158 us
    pallas_call x1, Pallas kernels: 159 us -> 148 us  [call_main(): pl.pallas_call(functools.partial(main_body, (nb, nm, na, T, S, CH, HC), n...]
where the time goes in v2:
time: 159 us
  Pallas kernels  158 us (99%)
    pallas_call x1, Pallas kernels, call_main(): pl.pallas_call(functools.partial(main_body, (nb, nm, na, T, S, CH, HC), n...  148 us
    pallas_call x1, Pallas kernels, call_last(): pl.pallas_call(functools.partial(last_body, (CH, total_in)), out_shape=bi...  10.6 us

profile of v2, /device:TPU:0, one launch (start us, length us, event | category | flops | bytes accessed | tf_op | source)
XLA Modules:
  0.0 159.1 jit_solution(12732942663632675104)
XLA Ops:
  0.6 147.7 %forward_and_backward.1 = (bf16[2048,768]{1,0:T(8,128)(2,1)}, bf16[2,2048,384]{2,1,0:T(8,128)(2,1)}, bf16[2,1024,384]{2,1,0:T(8,128)(2,1)}, bf16[5,768,384]{2,1,...) custom-call(bf16[4096,384]{1,0:T(8,128)(2,1)} %bitcast.6, s32[16,1024]{1,0:T(8,128)} %refs_1_.1, ...), custom_call_target="tpu_custom_call" | custom-call | flops 44000002048 | bytes 40000000 | tf_op jit(solution)/shard_map/forward_and_backward/pallas_call | solution.py:1248
  148.4 10.6 %last_pass.1 = (f32[16,256,384]{2,1,0:T(8,128)}, bf16[16,128,384]{2,1,0:T(8,128)(2,1)}, f32[5,768,384]{2,1,0:T(8,128)}, f32[576,768]{1,0:T(8,128)}, f32[384,384]...) custom-call(bf16[16,256,384]{2,1,0:T(8,128)(2,1)} %sig.1, ...), custom_call_target="tpu_custom_call" | custom-call | tf_op jit(solution)/shard_map/last_pass/pallas_call | solution.py:1403

commit v3 on v2

--- a/solution.py
+++ b/solution.py
@@ -1286,11 +1286,11 @@
     ld_st = load(stats, st_v, taps + 6)
     ld_dp = load(dp, dp_v, taps + 7)
     ld_st.start()
-    for k in range(taps):
-        load_tap(k).start()
     for h in range(2):
         for c in load_half(h):
             c.start()
+    for k in range(taps):
+        load_tap(k).start()
     ld_dp.start()
 
     def store_tap(k):
@@ -1308,7 +1308,6 @@
         store_tap(k).start()
         return 0
 
-    lax.fori_loop(0, taps, tap, 0)
     ld_st.wait()
     st = st_v[:, pl.ds(al(m * CH, CH), CH)]
     mu, inv, gain, gg, gb = [st[i : i + 1] for i in (0, 1, 2, 4, 5)]
@@ -1360,6 +1359,7 @@
         return 0
 
     lax.fori_loop(0, 2, half, 0)
+    lax.fori_loop(0, taps, tap, 0)
     ld_dp.wait()
     for k, at in enumerate((0, 6, 2)):
         for h in range(2):

time: 159 us -> 158 us (level)
  no operation moved by 1% of the time
where the time goes in v3:
time: 158 us
  Pallas kernels  157 us (99%)
    pallas_call x1, Pallas kernels, call_main(): pl.pallas_call(functools.partial(main_body, (nb, nm, na, T, S, CH, HC), n...  148 us
    pallas_call x1, Pallas kernels, call_last(): pl.pallas_call(functools.partial(last_body, (CH, total_in)), out_shape=bi...  9.6 us

profile of v3, /device:TPU:0, one launch (start us, length us, event | category | flops | bytes accessed | tf_op | source)
XLA Modules:
  0.0 158.2 jit_solution(17961889546547905461)
XLA Ops:
  0.6 147.7 %forward_and_backward.1 = (bf16[2048,768]{1,0:T(8,128)(2,1)}, bf16[2,2048,384]{2,1,0:T(8,128)(2,1)}, bf16[2,1024,384]{2,1,0:T(8,128)(2,1)}, bf16[5,768,384]{2,1,...) custom-call(bf16[4096,384]{1,0:T(8,128)(2,1)} %bitcast.6, s32[16,1024]{1,0:T(8,128)} %refs_1_.1, ...), custom_call_target="tpu_custom_call" | custom-call | flops 44000002048 | bytes 40000000 | tf_op jit(solution)/shard_map/forward_and_backward/pallas_call | solution.py:1248
  148.4 9.6 %last_pass.1 = (f32[16,256,384]{2,1,0:T(8,128)}, bf16[16,128,384]{2,1,0:T(8,128)(2,1)}, f32[5,768,384]{2,1,0:T(8,128)}, f32[576,768]{1,0:T(8,128)}, f32[384,384]...) custom-call(bf16[16,256,384]{2,1,0:T(8,128)(2,1)} %sig.1, ...), custom_call_target="tpu_custom_call" | custom-call | tf_op jit(solution)/shard_map/last_pass/pallas_call | solution.py:1403
